TPU v7x, 32 devices: a whole 2x2x4 slice. The times are simulated.
32 devices in a mesh: band: 4 (over y, core), plane: 8 (over z, x).
Axes of the slice: x: 2, y: 2, z: 4, core: 2. Of those that a mesh axis runs over, the one named last changes fastest.
Arguments:
- psi: float32 [2, 4, 4096, 128], P(None, 'band', 'plane'), may hold values from -8 to 8
- potential: float32 [96, 9216], P('plane'), may hold values from 0 to 2
- stick_column: int32 [4096], P('plane'), may hold values from 0 to 9215, as said below
- stick_length: int32 [4096], P('plane'), may hold values from 0 to 49, as said below
Outputs:
- psi_new: float32 [2, 4, 4096, 128], P(None, 'band', 'plane')
- potential_new: float32 [96, 9216], P('plane')
Inputs may be any that keep to these rules, and one draw needn't show every extreme that they name: `stick_column`: within each device's block of 512 slots the live sticks come first and the other slots are empty with column 0. Over all devices the live slots hold every column (mx mod 96) * 96 + (my mod 96) with mx * mx + my * my <= 576 exactly once, in an order drawn from the seed; some device's block is full and the others hold fewer. `stick_length`: A live slot's length is 2 h + 1, with h the largest whole number such that mx * mx + my * my + h * h <= 576 for its column; empty slots have length 0.
All inputs are finite; a program needn't handle non-finite values.
Results may differ from a plain program's by a relative error of at most 0.0001.
Values sent between devices are 32-bit elements; how exact they have to be, the bound alone decides.
A program may use at most 64 MiB of HBM per device.

v0:
```python
import functools
import math

import jax
import jax.numpy as jnp
import numpy as np
from jax import lax
from jax.experimental import pallas as pl
from jax.experimental.pallas import tpu as pltpu
from jax.sharding import PartitionSpec as P

NG = 96
RAD = 24
STICK_COEFFS = 128
BAND_DEV = 1
SIDE = 2 * RAD + 1
KY = 64
KX = 64
KZ = 56
LANE = 128

HIGHEST = lax.Precision.HIGHEST
TIMESTEP = 0.6
LINEAR_GAIN = 0.5
CUBIC_GAIN = 0.3


def turning(values):
    return values.astype(jnp.float32) * (2.0 * math.pi / NG)


def signed(index):
    return jnp.where(index > NG // 2, index - NG, index)


def height_tables(lengths, planes, device_list):
    order = jnp.arange(STICK_COEFFS, dtype=jnp.int32)
    height = (
        jnp.arange(device_list, dtype=jnp.int32)[None, :] * planes
        + jnp.arange(planes, dtype=jnp.int32)[:, None]
    )
    half = (lengths - 1) // 2
    shift_angle = -turning(height.T[:, :, None] * half[None, None, :] % NG)
    shift = (jnp.cos(shift_angle), jnp.sin(shift_angle))
    mask = (order[None, :] < lengths[:, None]).astype(jnp.float32)
    return (shift, mask)


def wave_table():
    angle = 2.0 * np.pi * (np.outer(np.arange(STICK_COEFFS), np.arange(NG)) % NG) / NG
    return ((np.cos(angle) * NG**-0.5).astype(np.float32), (np.sin(angle) * NG**-0.5).astype(np.float32))


def row_layout(device_list):
    half = [math.isqrt(RAD * RAD - (i - RAD) ** 2) for i in range(SIDE)]
    lanes = -(-sum(2 * h + 1 for h in half) // device_list)
    lanes = -(-lanes // LANE) * LANE
    order = sorted(range(SIDE), key=lambda i: (-half[i], i))
    while True:
        used = [0] * device_list
        place = [None] * SIDE
        for i in order:
            device = min(range(device_list), key=lambda d: (used[d], d))
            place[i] = (device, used[device])
            used[device] += 2 * half[i] + 1
        if max(used) <= lanes:
            return half, place, lanes
        lanes += LANE


def height_table(planes, device_list):
    freq = np.arange(KZ) - RAD
    angle = 2.0 * np.pi * (np.outer(np.arange(NG), freq) % NG) / NG
    keep = (np.arange(KZ) < SIDE) * NG**-0.5
    cosine = np.cos(angle) * keep
    sine = np.sin(angle) * keep
    table = np.block([[cosine, -sine], [sine, cosine]]).reshape(2, device_list, planes, 2 * KZ)
    return np.ascontiguousarray(table.transpose(1, 0, 2, 3).reshape(2 * NG, 2 * KZ)).astype(np.float32)


def plane_tables():
    freq = np.arange(KX) - RAD
    angle = 2.0 * np.pi * (np.outer(freq, np.arange(NG)) % NG) / NG
    keep = (np.arange(KX) < SIDE)[:, None] * NG**-0.5
    cosine = np.cos(angle) * keep
    sine = np.sin(angle) * keep
    inner = np.concatenate([cosine, sine], axis=0).T
    outer = np.concatenate([cosine, sine], axis=1)
    lines = np.zeros((LANE, 2, LANE))
    lines[:KY, 0, :NG] = cosine
    lines[:KY, 1, :NG] = sine
    back = np.zeros((2, LANE, 2, LANE))
    back[0, :NG, 0, :KY] = cosine.T
    back[1, :NG, 0, :KY] = sine.T
    back[0, :NG, 1, :KY] = -sine.T
    back[1, :NG, 1, :KY] = cosine.T
    return (
        np.ascontiguousarray(inner).astype(np.float32),
        outer.astype(np.float32),
        lines.reshape(LANE, 2 * LANE).astype(np.float32),
        back.reshape(2 * LANE, 2 * LANE).astype(np.float32),
    )


def thirds(values):
    first = values.astype(jnp.bfloat16).astype(jnp.float32)
    rest = values - first
    second = rest.astype(jnp.bfloat16).astype(jnp.float32)
    return jnp.concatenate([first, second, rest - second], axis=0).astype(jnp.bfloat16)


def add_thirds(parts):
    rows = parts.shape[0] // 3
    return parts[:rows] + parts[rows : 2 * rows] + parts[2 * rows :]


def spread_kernel(cells_ref, values_ref, out_ref):
    groups, rows, lanes = out_ref.shape
    slots = cells_ref.shape[1]
    index = lax.broadcasted_iota(jnp.int32, (slots, groups * lanes), 1)
    hits = jnp.where(index == cells_ref[0], 1.0, 0.0).astype(jnp.bfloat16)

    @pl.when(pl.program_id(0) == 0)
    def _():
        out_ref[...] = jnp.zeros_like(out_ref)

    parts = jnp.dot(thirds(values_ref[0]), hits, preferred_element_type=jnp.float32)
    whole = add_thirds(parts)
    for group in range(groups):
        out_ref[group] += whole[:rows, group * lanes : (group + 1) * lanes]


def pick_kernel(cells_ref, values_ref, out_ref):
    slots = cells_ref.shape[2]
    index = lax.broadcasted_iota(jnp.int32, (values_ref.shape[1], slots), 0)
    hits = jnp.where(index == cells_ref[0], 1.0, 0.0).astype(jnp.bfloat16)
    parts = jnp.dot(thirds(values_ref[...]), hits, preferred_element_type=jnp.float32)
    out_ref[0] = add_thirds(parts)[: out_ref.shape[1]]


def spread(cells, values, groups, lanes):
    sources, rows, slots = values.shape
    padded = -(-rows // 8) * 8
    values = jnp.pad(values, ((0, 0), (0, padded - rows), (0, 0)))
    return pl.pallas_call(
        spread_kernel,
        grid=(sources,),
        in_specs=[
            pl.BlockSpec((1, slots, 1), lambda i: (i, 0, 0)),
            pl.BlockSpec((1, padded, slots), lambda i: (i, 0, 0)),
        ],
        out_specs=pl.BlockSpec((groups, rows, lanes), lambda i: (0, 0, 0)),
        out_shape=jax.ShapeDtypeStruct((groups, rows, lanes), jnp.float32),
        compiler_params=pltpu.CompilerParams(vmem_limit_bytes=40 << 20),
    )(cells[:, :, None], values)


def pick(cells, values):
    sources, slots = cells.shape
    rows, count = values.shape
    padded = -(-rows // 8) * 8
    values = jnp.pad(values, ((0, padded - rows), (0, 0)))
    return pl.pallas_call(
        pick_kernel,
        grid=(sources,),
        in_specs=[
            pl.BlockSpec((1, 1, slots), lambda i: (i, 0, 0)),
            pl.BlockSpec((padded, count), lambda i: (0, 0)),
        ],
        out_specs=pl.BlockSpec((1, rows, slots), lambda i: (i, 0, 0)),
        out_shape=jax.ShapeDtypeStruct((sources, rows, slots), jnp.float32),
        compiler_params=pltpu.CompilerParams(vmem_limit_bytes=40 << 20),
    )(cells[:, None, :], values)


def product(left, right):
    return jnp.dot(left, right, precision=HIGHEST, preferred_element_type=jnp.float32)


def halves(values):
    first = values.astype(jnp.bfloat16)
    return first, (values - first.astype(jnp.float32)).astype(jnp.bfloat16)


def product_halves(left, right):
    def one(a, b):
        return jnp.dot(a, b, preferred_element_type=jnp.float32)

    return one(left[0], right[0]) + (one(left[0], right[1]) + one(left[1], right[0]))


def plane_kernel(layout, pitch, with_modulus, with_back, *refs):
    half, place, _ = layout
    arrived_ref, local_ref, inner_ref, outer_ref, lines_ref, back_ref = refs[:6]
    refs = refs[6:]
    if with_back:
        out_ref, refs = refs[0], refs[1:]
    if with_modulus:
        modulus_ref, refs = refs[0], refs[1:]
    box, cosine_part, sine_part = refs
    planes = local_ref.shape[0]
    rows = 2 * planes
    box[...] = jnp.zeros_like(box)
    for i in range(SIDE):
        device, lane = place[i]
        width = 2 * half[i] + 1
        box[i * pitch : i * pitch + rows, RAD - half[i] : RAD + half[i] + 1] = arrived_ref[
            device, :, lane : lane + width
        ]
    inner, outer = halves(inner_ref[...]), halves(outer_ref[...])
    turned = product_halves(halves(box[...]), halves(lines_ref[...]))
    cosine_part[...] = turned[:, :LANE]
    sine_part[...] = turned[:, LANE:]
    group = max(size for size in range(1, 5) if planes % size == 0)
    for begin in range(0, planes, group):
        top, bottom = [], []
        for p in range(begin, begin + group):
            real = pl.ds(p, KX, stride=pitch)
            imag = pl.ds(planes + p, KX, stride=pitch)
            line_real = cosine_part[real, :] - sine_part[imag, :]
            line_imag = sine_part[real, :] + cosine_part[imag, :]
            top += [line_real, line_imag]
            bottom += [-line_imag, line_real]
        lines = jnp.concatenate(
            [jnp.concatenate(top, axis=1), jnp.concatenate(bottom, axis=1)], axis=0
        )
        field = product_halves(inner, halves(lines))
        top, bottom = [], []
        for q in range(group):
            p = begin + q
            field_real = field[:, 2 * q * LANE : (2 * q + 1) * LANE]
            field_imag = field[:, (2 * q + 1) * LANE : (2 * q + 2) * LANE]
            if with_modulus:
                modulus_ref[p] = field_real * field_real + field_imag * field_imag
            if with_back:
                field_real = field_real * local_ref[p]
                field_imag = field_imag * local_ref[p]
                top += [field_real, field_imag]
                bottom += [field_imag, -field_real]
        if with_back:
            both = jnp.concatenate(
                [jnp.concatenate(top, axis=1), jnp.concatenate(bottom, axis=1)], axis=0
            )
            result = product_halves(outer, halves(both))
            result = jnp.concatenate(
                [result[:, 2 * q * LANE : (2 * q + 2) * LANE] for q in range(group)], axis=0
            )
            result = product_halves(halves(result), halves(back_ref[...]))
            for q in range(group):
                p = begin + q
                part = result[q * KX : (q + 1) * KX]
                box[pl.ds(p, KX, stride=pitch), :] = part[:, :LANE]
                box[pl.ds(planes + p, KX, stride=pitch), :] = part[:, LANE:]
    if with_back:
        out_ref[...] = jnp.zeros_like(out_ref)
        for i in range(SIDE):
            device, lane = place[i]
            width = 2 * half[i] + 1
            out_ref[device, :, lane : lane + width] = box[
                i * pitch : i * pitch + rows, RAD - half[i] : RAD + half[i] + 1
            ]


def plane_step(layout, arrived, local, tables, with_modulus, with_back):
    planes = local.shape[0]
    pitch = -(-2 * planes // 8) * 8
    shapes = []
    if with_back:
        shapes.append(jax.ShapeDtypeStruct(arrived.shape, jnp.float32))
    if with_modulus:
        shapes.append(jax.ShapeDtypeStruct(local.shape, jnp.float32))
    kernel = functools.partial(plane_kernel, layout, pitch, with_modulus, with_back)
    whole = pl.BlockSpec(memory_space=pltpu.VMEM)
    return pl.pallas_call(
        kernel,
        in_specs=[whole] * 6,
        out_specs=[whole] * len(shapes),
        out_shape=shapes,
        scratch_shapes=[pltpu.VMEM((KX * pitch, LANE), jnp.float32)] * 3,
        compiler_params=pltpu.CompilerParams(vmem_limit_bytes=40 << 20),
    )(arrived, local, *tables)


def height_kernel(factor, last, returned_ref, term_ref, total_ref, kinetic_ref, inside_ref, table_ref, turned_ref, *refs):
    table = table_ref[...]
    applied = product(turned_ref[...], returned_ref[...]) * inside_ref[...]
    applied = applied + kinetic_ref[...] * term_ref[...]
    term = factor * jnp.concatenate([applied[KZ:], -applied[:KZ]], axis=0)
    total = total_ref[...] + term
    refs[0][...] = product(table, total if last else term)
    if not last:
        refs[1][...] = term
        refs[2][...] = total


def height_step(factor, last, returned, term, total, kinetic, inside, table):
    lanes = term.shape[1]
    shapes = [jax.ShapeDtypeStruct((table.shape[0], lanes), jnp.float32)]
    if not last:
        shapes += [jax.ShapeDtypeStruct(term.shape, jnp.float32)] * 2
    whole = pl.BlockSpec(memory_space=pltpu.VMEM)
    return pl.pallas_call(
        functools.partial(height_kernel, factor, last),
        in_specs=[whole] * 7,
        out_specs=[whole] * len(shapes),
        out_shape=shapes,
        compiler_params=pltpu.CompilerParams(vmem_limit_bytes=40 << 20),
    )(returned, term, total, kinetic, inside, table, np.ascontiguousarray(table.T))


def dot(subscripts, left, right):
    return jnp.einsum(subscripts, left, right, precision=HIGHEST)


def sum_bands(values):
    bands = lax.axis_size("band")
    if bands & (bands - 1):
        return lax.psum(values, "band")
    step = 1
    while step < bands:
        pairs = [(i, i ^ step) for i in range(bands)]
        values = values + lax.ppermute(values, "band", pairs)
        step *= 2
    return values


def shards(psi, potential, stick_column, stick_length):
    device_list = lax.axis_size("plane")
    planes = potential.shape[0]
    slots = stick_column.shape[0]
    layout = row_layout(device_list)
    half, place, lanes = layout
    wave = wave_table()
    shift, mask = height_tables(stick_length, planes, device_list)

    def exchange(values):
        return lax.all_to_all(values, "plane", split_axis=0, concat_axis=0, tiled=True)

    term = psi[:, 0] * mask
    upper = [
        dot("sj,jz->zs", term[0], wave[0]) - dot("sj,jz->zs", term[1], wave[1]),
        dot("sj,jz->zs", term[0], wave[1]) + dot("sj,jz->zs", term[1], wave[0]),
    ]
    upper = [part.reshape(device_list, planes, slots) for part in upper]
    first = signed(stick_column // NG)
    second = signed(stick_column % NG)
    base = np.array([place[i][0] * lanes + place[i][1] + half[i] for i in range(SIDE)], np.int32)
    chosen = first[None, :] + RAD == jnp.arange(SIDE, dtype=jnp.int32)[:, None]
    own_cell = jnp.sum(jnp.where(chosen, base[:, None], 0), axis=0) + second
    own_cell = jnp.where(stick_length > 0, own_cell, -1)
    packed = jnp.concatenate(
        [
            upper[0] * shift[0] - upper[1] * shift[1],
            upper[0] * shift[1] + upper[1] * shift[0],
            jnp.broadcast_to(own_cell.astype(jnp.float32), (device_list, 1, slots)),
        ],
        axis=1,
    )
    arrived = exchange(packed)
    cells = arrived[:, 2 * planes, :].astype(jnp.int32)
    start = spread(cells, arrived[:, : 2 * planes, :], device_list, lanes)

    local = jnp.pad(potential.reshape(planes, NG, NG), ((0, 0), (0, 0), (0, LANE - NG)))
    tables = plane_tables()
    table = height_table(planes, device_list)
    planar = np.full((device_list, lanes), 4 * RAD * RAD, np.int32)
    for i in range(SIDE):
        device, lane = place[i]
        spot = np.arange(-half[i], half[i] + 1)
        planar[device, lane : lane + 2 * half[i] + 1] = (i - RAD) ** 2 + spot * spot
    planar = lax.dynamic_slice_in_dim(jnp.asarray(planar), lax.axis_index("plane"), 1, 0)
    depth = np.concatenate([np.arange(KZ) - RAD] * 2).astype(np.int32)[:, None]
    square = planar + depth * depth
    inside = (square <= RAD * RAD).astype(jnp.float32)
    kinetic = square.astype(jnp.float32) / (RAD * RAD) * inside

    spectrum, before = plane_step(layout, start, local, tables, True, True)
    returned = exchange(jnp.concatenate([spectrum, start], axis=1))
    shape = (2 * NG, lanes)
    term = dot("zk,zl->kl", table, returned[:, 2 * planes :].reshape(shape)) * inside
    total = term
    returned = returned[:, : 2 * planes]
    for power in range(1, 4):
        if power > 1:
            (spectrum,) = plane_step(layout, exchange(upper.reshape(start.shape)), local, tables, False, True)
            returned = exchange(spectrum)
        made = height_step(
            TIMESTEP / power, power == 3, returned.reshape(shape), term, total, kinetic, inside, table
        )
        if power < 3:
            upper, term, total = made
        else:
            upper = made[0]
    final = exchange(upper.reshape(start.shape))
    (after,) = plane_step(layout, final, local, tables, True, False)
    flat = final.transpose(1, 0, 2).reshape(2 * planes, device_list * lanes)
    home = exchange(pick(cells, flat))
    real, imag = home[:, :planes], home[:, planes:]
    turned = [
        (real * shift[0] + imag * shift[1]).reshape(NG, slots),
        (imag * shift[0] - real * shift[1]).reshape(NG, slots),
    ]
    psi_new = jnp.stack(
        [
            (dot("zs,jz->sj", turned[0], wave[0]) + dot("zs,jz->sj", turned[1], wave[1])) * mask,
            (dot("zs,jz->sj", turned[1], wave[0]) - dot("zs,jz->sj", turned[0], wave[1])) * mask,
        ]
    )[:, None]
    change = (after - before)[..., :NG].reshape(planes, NG * NG) / BAND_DEV
    whole = sum_bands(change)
    potential_new = potential + LINEAR_GAIN * whole + CUBIC_GAIN * whole * whole * whole
    return (psi_new, potential_new)


def solution(mesh):
    in_specs = (P(None, "band", "plane", None), P("plane", None), P("plane"), P("plane"))
    out_specs = (P(None, "band", "plane", None), P("plane", None))
    return jax.shard_map(shards, mesh=mesh, in_specs=in_specs, out_specs=out_specs, check_vma=False)
```

profile of v0, /device:TPU:0, one launch (start us, length us, event | category | flops | bytes accessed | tf_op | source)
XLA Modules:
  0.0 157.6 jit_solution(2910461397615549771)
XLA Ops:
  0.7 0.7 fusion.22
  1.4 0.8 fusion.14
  2.2 0.8 select_reduce_fusion
  3.0 0.7 add_select_fusion.3
  3.7 1.1 bitcast_multiply_fusion
  4.8 1.3 fusion.16
  6.1 0.4 fusion.17
  6.5 0.4 fusion.4
  7.0 0.4 fusion.5
  7.5 1.3 multiply_subtract_fusion.1
  8.8 0.9 pad_maximum_fusion
  9.7 7.3 %all-to-all-start = ((f32[8,25,512]{2,1,0:T(8,128)}), f32[8,25,512]{2,1,0:T(8,128)}, u32[]{:S(2)}, u32[]{:S(2)}) async-start(f32[8,25,512]{2,1,0:T(8,128)} %pad_maximum_fusion), calls=%async_computation | async-start | bytes 1048576 | tf_op jit(solution)/shard_map/all_to_all | solution.py:337
  17.2 14.3 %all-to-all-done = f32[8,25,512]{2,1,0:T(8,128)} async-done(((f32[8,25,512]{2,1,0:T(8,128)}), f32[8,25,512]{2,1,0:T(8,128)}, u32[]{:S(2)}, u32[]{:S(2)}) %all-to-all-start) | async-done | bytes 409632 | tf_op jit(solution)/shard_map/all_to_all | solution.py:337
  31.5 0.9 fusion.28
  32.5 0.6 copy.31.cells_ref
  33.1 1.1 slice.41.values_ref
  34.2 8.5 %shard_map.239.refs_0_ = f32[8,24,256]{2,1,0:T(8,128)S(1)} custom-call(s32[8,512,1]{2,1,0:T(8,128)S(1)} %copy.31.cells_ref, f32[8,24,512]{2,1,0:T(8,128)S(1)} %slice.41.values_ref), custom_call_target="tpu_custom_call" | custom-call | tf_op jit(solution)/shard_map/pallas_call | solution.py:145
  42.8 4.2 %shard_map.240 = (f32[8,24,256]{2,1,0:T(8,128)S(1)}, f32[12,96,128]{2,1,0:T(8,128)S(1)}) custom-call(f32[8,24,256]{2,1,0:T(8,128)S(1)} %shard_map.239.refs_0_, f32[12,96,128]{2,1,0:T(8,128)S(1)} %pad.4.refs_1_, f32[96,128]{1,0:T(8,128)S(1)} %copy-done.5, f32[64,192]{1,0:T(8,128)S(1)} %copy-done.3, f32[128,256]{1,0:T(8,128)S(1)} %copy-done.1, ...), custom_call_target="tpu_custom_call" | custom-call | tf_op jit(solution)/shard_map/pallas_call | solution.py:274
  47.0 0.8 pad_maximum_fusion.1
  47.8 3.7 %all-to-all-start.1 = ((f32[8,48,256]{2,1,0:T(8,128)}), f32[8,48,256]{2,1,0:T(8,128)S(1)}, u32[]{:S(2)}, u32[]{:S(2)}) async-start(f32[8,48,256]{2,1,0:T(8,128)} %pad_maximum_fusion.1), calls=%async_computation.1 | async-start | bytes 786432 | tf_op jit(solution)/shard_map/all_to_all | solution.py:337
  51.4 0.7 constant_dynamic-slice_fusion
  52.3 11.0 %all-to-all-done.1 = f32[8,48,256]{2,1,0:T(8,128)S(1)} async-done(((f32[8,48,256]{2,1,0:T(8,128)}), f32[8,48,256]{2,1,0:T(8,128)S(1)}, u32[]{:S(2)}, u32[]{:S(2)}) %all-to-all-start.1) | async-done | bytes 393248 | tf_op jit(solution)/shard_map/all_to_all | solution.py:337
  63.3 0.4 convolution_select_fusion.term_ref.total_ref
  63.7 0.7 shard_map.241
  64.5 11.5 %all_to_all.40.refs_0_ = f32[8,24,256]{2,1,0:T(8,128)S(1)} all-to-all(f32[8,24,256]{2,1,0:T(8,128)S(1)} %bitcast.56), channel_id=1, replica_groups=mesh['band'=4,'plane'=8] {'plane'}, dimensions={0} | all-to-all | bytes 393216 | tf_op jit(solution)/shard_map/all_to_all | solution.py:337
  75.9 4.2 %shard_map.242 = f32[8,24,256]{2,1,0:T(8,128)S(1)} custom-call(f32[8,24,256]{2,1,0:T(8,128)S(1)} %all_to_all.40.refs_0_, f32[12,96,128]{2,1,0:T(8,128)S(1)} %pad.4.refs_1_, f32[96,128]{1,0:T(8,128)S(1)} %copy-done.5, f32[64,192]{1,0:T(8,128)S(1)} %copy-done.3, f32[128,256]{1,0:T(8,128)S(1)} %copy-done.1, f32[256,256]{1,0:T(8,128)S(1)} %copy-done), custom_call_target="tpu_custom_call" | custom-call | tf_op jit(solution)/shard_map/pallas_call | solution.py:274
  80.1 10.7 %all_to_all.41 = f32[8,24,256]{2,1,0:T(8,128)S(1)} all-to-all(f32[8,24,256]{2,1,0:T(8,128)S(1)} %shard_map.242), channel_id=1, replica_groups=mesh['band'=4,'plane'=8] {'plane'}, dimensions={0} | all-to-all | bytes 393216 | tf_op jit(solution)/shard_map/all_to_all | solution.py:337
  90.9 0.7 shard_map.243
  91.6 10.6 %all_to_all.42.refs_0_ = f32[8,24,256]{2,1,0:T(8,128)S(1)} all-to-all(f32[8,24,256]{2,1,0:T(8,128)S(1)} %bitcast.55), channel_id=1, replica_groups=mesh['band'=4,'plane'=8] {'plane'}, dimensions={0} | all-to-all | bytes 393216 | tf_op jit(solution)/shard_map/all_to_all | solution.py:337
  102.2 4.2 %shard_map.244 = f32[8,24,256]{2,1,0:T(8,128)S(1)} custom-call(f32[8,24,256]{2,1,0:T(8,128)S(1)} %all_to_all.42.refs_0_, f32[12,96,128]{2,1,0:T(8,128)S(1)} %pad.4.refs_1_, f32[96,128]{1,0:T(8,128)S(1)} %copy-done.5, f32[64,192]{1,0:T(8,128)S(1)} %copy-done.3, f32[128,256]{1,0:T(8,128)S(1)} %copy-done.1, f32[256,256]{1,0:T(8,128)S(1)} %copy-done), custom_call_target="tpu_custom_call" | custom-call | tf_op jit(solution)/shard_map/pallas_call | solution.py:274
  106.4 10.5 %all_to_all.43 = f32[8,24,256]{2,1,0:T(8,128)S(1)} all-to-all(f32[8,24,256]{2,1,0:T(8,128)S(1)} %shard_map.244), channel_id=1, replica_groups=mesh['band'=4,'plane'=8] {'plane'}, dimensions={0} | all-to-all | bytes 393216 | tf_op jit(solution)/shard_map/all_to_all | solution.py:337
  116.8 0.7 shard_map.245
  117.6 10.2 %all_to_all.44.refs_0_ = f32[8,24,256]{2,1,0:T(8,128)S(1)} all-to-all(f32[8,24,256]{2,1,0:T(8,128)S(1)} %bitcast.51), channel_id=1, replica_groups=mesh['band'=4,'plane'=8] {'plane'}, dimensions={0} | all-to-all | bytes 393216 | tf_op jit(solution)/shard_map/all_to_all | solution.py:337
  127.8 5.0 %shard_map.246 = f32[8,24,512]{2,1,0:T(8,128)} custom-call(s32[8,1,512]{2,1,0:T(1,128)S(1)} %get-tuple-element.27.cells_ref, f32[24,2048]{1,0:T(8,128)S(1)} %bitcast.53), custom_call_target="tpu_custom_call" | custom-call | tf_op jit(solution)/shard_map/pallas_call | solution.py:163
  132.8 3.5 %all-to-all-start.7 = ((f32[8,24,512]{2,1,0:T(8,128)}), f32[8,24,512]{2,1,0:T(8,128)S(1)}, u32[]{:S(2)}, u32[]{:S(2)}) async-start(f32[8,24,512]{2,1,0:T(8,128)} %shard_map.246), calls=%async_computation.7 | async-start | bytes 786432 | tf_op jit(solution)/shard_map/all_to_all | solution.py:337
  136.2 2.4 %shard_map.247 = f32[12,96,128]{2,1,0:T(8,128)S(1)} custom-call(f32[8,24,256]{2,1,0:T(8,128)S(1)} %all_to_all.44.refs_0_, f32[12,96,128]{2,1,0:T(8,128)S(1)} %pad.4.refs_1_, f32[96,128]{1,0:T(8,128)S(1)} %copy-done.5, f32[64,192]{1,0:T(8,128)S(1)} %copy-done.3, f32[128,256]{1,0:T(8,128)S(1)} %copy-done.1, f32[256,256]{1,0:T(8,128)S(1)} %copy-done), custom_call_target="tpu_custom_call" | custom-call | tf_op jit(solution)/shard_map/pallas_call | solution.py:274
  138.7 0.3 reshape.116
  139.1 2.0 %collective-permute-done = f32[12,9216]{1,0:T(8,128)S(1)} collective-permute-done((f32[12,9216]{1,0:T(8,128)S(1)}, f32[12,9216]{1,0:T(8,128)S(1)}, u32[]{:S(2)}, u32[]{:S(2)}) %collective-permute-start) | collective-permute-done | bytes 442400 | tf_op jit(solution)/shard_map/ppermute | solution.py:322
  141.2 1.6 collective-permute-start.1
  142.8 2.6 %all-to-all-done.7 = f32[8,24,512]{2,1,0:T(8,128)S(1)} async-done(((f32[8,24,512]{2,1,0:T(8,128)}), f32[8,24,512]{2,1,0:T(8,128)S(1)}, u32[]{:S(2)}, u32[]{:S(2)}) %all-to-all-start.7) | async-done | bytes 393248 | tf_op jit(solution)/shard_map/all_to_all | solution.py:337
  145.4 1.3 multiply_add_fusion
  146.7 0.6 fusion.31
  147.4 0.6 fusion.30
  148.0 0.6 fusion.1
  148.6 0.6 fusion.3
  149.2 0.8 maximum_bitcast_fusion
  150.0 6.6 %collective-permute-done.1 = f32[12,9216]{1,0:T(8,128)S(1)} collective-permute-done((f32[12,9216]{1,0:T(8,128)S(1)}, f32[12,9216]{1,0:T(8,128)S(1)}, u32[]{:S(2)}, u32[]{:S(2)}) %collective-permute-start.1) | collective-permute-done | bytes 442400 | tf_op jit(solution)/shard_map/ppermute | solution.py:322
  156.6 1.0 fusion.6
  (40 shorter events, 0.9 us)
Async XLA Ops:
  0.6 6.3 %copy-start.8 = (f32[128,96]{1,0:T(8,128)S(1)}, f32[128,96]{1,0:T(8,128)}, u32[]{:S(2)}) copy-start(f32[128,96]{1,0:T(8,128)} %constant.97.clone) | copy-start | bytes 147460
  0.6 5.4 %copy-start.9 = (f32[128,96]{1,0:T(8,128)S(1)}, f32[128,96]{1,0:T(8,128)}, u32[]{:S(2)}) copy-start(f32[128,96]{1,0:T(8,128)} %constant.96.clone) | copy-start | bytes 147460
  7.0 10.0 %copy-start.6 = (f32[12,9216]{1,0:T(8,128)S(1)}, f32[12,9216]{1,0:T(8,128)}, u32[]{:S(2)}) copy-start(f32[12,9216]{1,0:T(8,128)} %param.25) | copy-start | bytes 1327108
  9.7 21.8 %all-to-all-start = ((f32[8,25,512]{2,1,0:T(8,128)}), f32[8,25,512]{2,1,0:T(8,128)}, u32[]{:S(2)}, u32[]{:S(2)}) async-start(f32[8,25,512]{2,1,0:T(8,128)} %pad_maximum_fusion), calls=%async_computation | async-start | bytes 1048576 | tf_op jit(solution)/shard_map/all_to_all | solution.py:337
  33.1 9.6 %copy-start = (f32[256,256]{1,0:T(8,128)S(1)}, f32[256,256]{1,0:T(8,128)}, u32[]{:S(2)}) copy-start(f32[256,256]{1,0:T(8,128)} %constant.104.clone.refs_5_) | copy-start | bytes 786436
  33.1 9.6 %copy-start.1 = (f32[128,256]{1,0:T(8,128)S(1)}, f32[128,256]{1,0:T(8,128)}, u32[]{:S(2)}) copy-start(f32[128,256]{1,0:T(8,128)} %constant.103.clone.refs_4_) | copy-start | bytes 393220
  33.1 9.6 %copy-start.3 = (f32[64,192]{1,0:T(8,128)S(1)}, f32[64,192]{1,0:T(8,128)}, u32[]{:S(2)}) copy-start(f32[64,192]{1,0:T(8,128)} %constant.102.clone.refs_3_) | copy-start | bytes 147460
  33.1 9.6 %copy-start.5 = (f32[96,128]{1,0:T(8,128)S(1)}, f32[96,128]{1,0:T(8,128)}, u32[]{:S(2)}) copy-start(f32[96,128]{1,0:T(8,128)} %constant.101.clone.refs_2_) | copy-start | bytes 147460
  42.8 9.4 %copy-start.11 = (s32[112]{0:T(128)S(1)}, s32[112]{0:T(128)}, u32[]{:S(2)}) copy-start(s32[112]{0:T(128)} %constant.112) | copy-start | bytes 1348
  42.8 20.5 %copy-start.2 = (f32[192,112]{1,0:T(8,128)S(1)}, f32[192,112]{1,0:T(8,128)}, u32[]{:S(2)}) copy-start(f32[192,112]{1,0:T(8,128)} %constant.105.clone.table_ref) | copy-start | bytes 258052
  42.8 21.0 %copy-start.4 = (f32[112,192]{1,0:T(8,128)S(1)}, f32[112,192]{1,0:T(8,128)}, u32[]{:S(2)}) copy-start(f32[112,192]{1,0:T(8,128)} %constant.106.clone.turned_ref) | copy-start | bytes 258052
  47.8 15.5 %all-to-all-start.1 = ((f32[8,48,256]{2,1,0:T(8,128)}), f32[8,48,256]{2,1,0:T(8,128)S(1)}, u32[]{:S(2)}, u32[]{:S(2)}) async-start(f32[8,48,256]{2,1,0:T(8,128)} %pad_maximum_fusion.1), calls=%async_computation.1 | async-start | bytes 786432 | tf_op jit(solution)/shard_map/all_to_all | solution.py:337
  132.8 12.6 %all-to-all-start.7 = ((f32[8,24,512]{2,1,0:T(8,128)}), f32[8,24,512]{2,1,0:T(8,128)S(1)}, u32[]{:S(2)}, u32[]{:S(2)}) async-start(f32[8,24,512]{2,1,0:T(8,128)} %shard_map.246), calls=%async_computation.7 | async-start | bytes 786432 | tf_op jit(solution)/shard_map/all_to_all | solution.py:337
  139.1 8.9 %copy-start.10 = (s32[512]{0:T(512)S(1)}, s32[512]{0:T(512)}, u32[]{:S(2)}) copy-start(s32[512]{0:T(512)} %param.27) | copy-start | bytes 6148
  139.1 2.1 %collective-permute-start = (f32[12,9216]{1,0:T(8,128)S(1)}, f32[12,9216]{1,0:T(8,128)S(1)}, u32[]{:S(2)}, u32[]{:S(2)}) collective-permute-start(f32[12,9216]{1,0:T(8,128)S(1)} %reshape.116), channel_id=1, source_target_pairs={{0,8},{8,0},{16,24},{24,16},{1,9},{9,1},{17,25},{25,17},{2,10},{10... | collective-permute-start | bytes 1327112 | tf_op jit(solution)/shard_map/ppermute | solution.py:322
  141.2 15.4 %collective-permute-start.1 = (f32[12,9216]{1,0:T(8,128)S(1)}, f32[12,9216]{1,0:T(8,128)S(1)}, u32[]{:S(2)}, u32[]{:S(2)}) collective-permute-start(f32[12,9216]{1,0:T(8,128)S(1)} %add.113), channel_id=1, source_target_pairs={{0,16},{8,24},{16,0},{24,8},{1,17},{9,25},{17,1},{25,9},{2,18},{10... | collective-permute-start | bytes 1327112 | tf_op jit(solution)/shard_map/ppermute | solution.py:322
  146.7 9.9 %copy-start.7 = (f32[12,9216]{1,0:T(8,128)S(1)}, f32[12,9216]{1,0:T(8,128)}, u32[]{:S(2)}) copy-start(f32[12,9216]{1,0:T(8,128)} %param.25) | copy-start | bytes 1327108
where the time goes:
time: 158 us
  blocking collectives  53.5 us (34%)
  waiting for transfers between devices  36.5 us (23%)
  Pallas kernels  30.5 us (19%)
  starting transfers between devices  16 us (10%)
  other arithmetic  11.4 us (7%)
  matrix products  5.32 us (3%)
  local copies, waits for them, and re-layouts  3.24 us (2%)
    all_to_all x5, blocking collectives, exchange(): lax.all_to_all(values, 'plane', split_axis=0, concat_axis=0, tiled=True)  53.5 us
    all_to_all x3, waiting for transfers between devices, exchange(): lax.all_to_all(values, 'plane', split_axis=0, concat_axis=0, tiled=True)  27.9 us
    pallas_call x4, Pallas kernels, plane_step(): pl.pallas_call(kernel, in_specs=[whole] * 6, out_specs=[whole] * len(shap...  14.9 us
    all_to_all x3, starting transfers between devices, exchange(): lax.all_to_all(values, 'plane', split_axis=0, concat_axis=0, tiled=True)  14.4 us
    ppermute x2, waiting for transfers between devices, sum_bands(): values = values + lax.ppermute(values, 'band', pairs)  8.6 us
    pallas_call x1, Pallas kernels, spread(): pl.pallas_call(spread_kernel, grid=(sources,), in_specs=[pl.BlockSpec((1,...  8.49 us
    dot_general x9, matrix products, dot(): return jnp.einsum(subscripts, left, right, precision=HIGHEST)  5.32 us
    pallas_call x1, Pallas kernels, pick(): pl.pallas_call(pick_kernel, grid=(sources,), in_specs=[pl.BlockSpec((1, 1...  5 us
  transfers between devices with their start and end apart: 5, of which 5 were waited for; matrix products, arithmetic and copies ran while one was open for 4% of the time, Pallas kernels for 2%

commit v1 on v0

--- a/solution.py
+++ b/solution.py
@@ -281,31 +281,94 @@
     )(arrived, local, *tables)
 
 
-def height_kernel(factor, last, returned_ref, term_ref, total_ref, kinetic_ref, inside_ref, table_ref, turned_ref, *refs):
-    table = table_ref[...]
-    applied = product(turned_ref[...], returned_ref[...]) * inside_ref[...]
-    applied = applied + kinetic_ref[...] * term_ref[...]
+def trade(count, sent, landed, send_sem, recv_sem):
+    me = lax.axis_index("plane")
+    band = lax.axis_index("band")
+    copies = []
+    for k in range(1, count):
+        partner = lax.rem(me + k, count)
+        copy = pltpu.make_async_remote_copy(
+            src_ref=sent.at[partner],
+            dst_ref=landed.at[me],
+            send_sem=send_sem.at[k - 1],
+            recv_sem=recv_sem.at[k - 1],
+            device_id=(band, partner),
+            device_id_type=pl.DeviceIdType.MESH,
+        )
+        copy.start()
+        copies.append(copy)
+    landed[me] = sent[me]
+    return copies
+
+
+def height_kernel(count, factor, opening, last, *refs):
+    spectrum_ref, term_ref, total_ref, kinetic_ref, inside_ref, table_ref, turned_ref = refs[:7]
+    outs, scratch = refs[7 : 8 if last else 10], refs[8 if last else 10 :]
+    landed, sent, final, flat, send_sem, recv_sem, send_later, recv_later = scratch[:8]
+    me = lax.axis_index("plane")
+    band = lax.axis_index("band")
+    barrier = pltpu.get_barrier_semaphore()
+    for k in range(1, count):
+        pl.semaphore_signal(
+            barrier,
+            inc=1,
+            device_id=(band, lax.rem(me + k, count)),
+            device_id_type=pl.DeviceIdType.MESH,
+        )
+    pl.semaphore_wait(barrier, count - 1)
+    copies = trade(count, spectrum_ref, landed, send_sem, recv_sem)
+    if opening:
+        origin, origin_send, origin_recv = scratch[8:]
+        copies += trade(count, term_ref, origin, origin_send, origin_recv)
+    for copy in copies:
+        copy.wait()
+    rows = landed.shape[1]
+    table, turned, inside = table_ref[...], turned_ref[...], inside_ref[...]
+
+    def gathered(buffer):
+        for d in range(count):
+            flat[d * rows : (d + 1) * rows, :] = buffer[d]
+        return product(turned, flat[...]) * inside
+
+    before = gathered(origin) if opening else term_ref[...]
+    total = before if opening else total_ref[...]
+    applied = gathered(landed) + kinetic_ref[...] * before
     term = factor * jnp.concatenate([applied[KZ:], -applied[:KZ]], axis=0)
-    total = total_ref[...] + term
-    refs[0][...] = product(table, total if last else term)
+    total = total + term
+    flat[...] = product(table, total if last else term)
+    for d in range(count):
+        sent[d] = flat[d * rows : (d + 1) * rows, :]
+    copies = trade(count, sent, final, send_later, recv_later)
     if not last:
-        refs[1][...] = term
-        refs[2][...] = total
-
-
-def height_step(factor, last, returned, term, total, kinetic, inside, table):
-    lanes = term.shape[1]
-    shapes = [jax.ShapeDtypeStruct((table.shape[0], lanes), jnp.float32)]
+        outs[1][...] = term
+        outs[2][...] = total
+    for copy in copies:
+        copy.wait()
+    outs[0][...] = final[...]
+
+
+def height_step(power, spectrum, term, total, kinetic, inside, table):
+    count, rows, lanes = spectrum.shape
+    opening, last = power == 1, power == 3
+    shapes = [jax.ShapeDtypeStruct(spectrum.shape, jnp.float32)]
     if not last:
-        shapes += [jax.ShapeDtypeStruct(term.shape, jnp.float32)] * 2
+        shapes += [jax.ShapeDtypeStruct((table.shape[1], lanes), jnp.float32)] * 2
     whole = pl.BlockSpec(memory_space=pltpu.VMEM)
+    block = pltpu.VMEM((count, rows, lanes), jnp.float32)
+    marks = pltpu.SemaphoreType.DMA((count - 1,))
     return pl.pallas_call(
-        functools.partial(height_kernel, factor, last),
+        functools.partial(height_kernel, count, TIMESTEP / power, opening, last),
         in_specs=[whole] * 7,
         out_specs=[whole] * len(shapes),
         out_shape=shapes,
-        compiler_params=pltpu.CompilerParams(vmem_limit_bytes=40 << 20),
-    )(returned, term, total, kinetic, inside, table, np.ascontiguousarray(table.T))
+        scratch_shapes=[block] * 3
+        + [pltpu.VMEM((count * rows, lanes), jnp.float32)]
+        + [marks] * 4
+        + ([block, marks, marks] if opening else []),
+        compiler_params=pltpu.CompilerParams(
+            vmem_limit_bytes=40 << 20, collective_id=power, has_side_effects=True
+        ),
+    )(spectrum, term, total, kinetic, inside, table, np.ascontiguousarray(table.T))
 
 
 def dot(subscripts, left, right):
@@ -375,23 +438,11 @@
     kinetic = square.astype(jnp.float32) / (RAD * RAD) * inside
 
     spectrum, before = plane_step(layout, start, local, tables, True, True)
-    returned = exchange(jnp.concatenate([spectrum, start], axis=1))
-    shape = (2 * NG, lanes)
-    term = dot("zk,zl->kl", table, returned[:, 2 * planes :].reshape(shape)) * inside
-    total = term
-    returned = returned[:, : 2 * planes]
-    for power in range(1, 4):
-        if power > 1:
-            (spectrum,) = plane_step(layout, exchange(upper.reshape(start.shape)), local, tables, False, True)
-            returned = exchange(spectrum)
-        made = height_step(
-            TIMESTEP / power, power == 3, returned.reshape(shape), term, total, kinetic, inside, table
-        )
-        if power < 3:
-            upper, term, total = made
-        else:
-            upper = made[0]
-    final = exchange(upper.reshape(start.shape))
+    arrived, term, total = height_step(1, spectrum, start, kinetic, kinetic, inside, table)
+    (spectrum,) = plane_step(layout, arrived, local, tables, False, True)
+    arrived, term, total = height_step(2, spectrum, term, total, kinetic, inside, table)
+    (spectrum,) = plane_step(layout, arrived, local, tables, False, True)
+    (final,) = height_step(3, spectrum, term, total, kinetic, inside, table)
     (after,) = plane_step(layout, final, local, tables, True, False)
     flat = final.transpose(1, 0, 2).reshape(2 * planes, device_list * lanes)
     home = exchange(pick(cells, flat))

time: 158 us -> 135 us (0.85)
  blocking collectives: 53.5 us -> 0 us
  Pallas kernels: 30.5 us -> 75.8 us
  waiting for transfers between devices: 36.5 us -> 24.8 us
  starting transfers between devices: 16 us -> 13.1 us
    all_to_all x5 -> x0, blocking collectives: 53.5 us -> none  [exchange(): lax.all_to_all(values, 'plane', split_axis=0, concat_axis=0, tiled=True)]
    pallas_call x3, Pallas kernels: 2.11 us -> 46.9 us  [height_step(): pl.pallas_call(functools.partial(height_kernel, count, TIMESTEP / power,...]
    all_to_all x3 -> x2, waiting for transfers between devices: 27.9 us -> 18.5 us  [exchange(): lax.all_to_all(values, 'plane', split_axis=0, concat_axis=0, tiled=True)]
    all_to_all x3 -> x2, starting transfers between devices: 14.4 us -> 11.5 us  [exchange(): lax.all_to_all(values, 'plane', split_axis=0, concat_axis=0, tiled=True)]
    ppermute x2, waiting for transfers between devices: 8.6 us -> 6.26 us  [sum_bands(): values = values + lax.ppermute(values, 'band', pairs)]
    dot_general x9 -> x8, matrix products: 5.32 us -> 4.92 us  [dot(): return jnp.einsum(subscripts, left, right, precision=HIGHEST)]
  transfers between devices with their start and end apart: 5 -> 4, of which waited for: 5 -> 4; matrix products, arithmetic and copies ran while one was open for 4% -> 5% of each run, Pallas kernels for 2% -> 0%
where the time goes in v1:
time: 135 us
  Pallas kernels  75.8 us (56%)
  waiting for transfers between devices  24.8 us (18%)
  starting transfers between devices  13.1 us (10%)
  other arithmetic  11.7 us (9%)
  matrix products  4.92 us (4%)
  local copies, waits for them, and re-layouts  3.23 us (2%)
    pallas_call x3, Pallas kernels, height_step(): pl.pallas_call(functools.partial(height_kernel, count, TIMESTEP / power,...  46.9 us
    all_to_all x2, waiting for transfers between devices, exchange(): lax.all_to_all(values, 'plane', split_axis=0, concat_axis=0, tiled=True)  18.5 us
    pallas_call x4, Pallas kernels, plane_step(): pl.pallas_call(kernel, in_specs=[whole] * 6, out_specs=[whole] * len(shap...  15.2 us
    all_to_all x2, starting transfers between devices, exchange(): lax.all_to_all(values, 'plane', split_axis=0, concat_axis=0, tiled=True)  11.5 us
    pallas_call x1, Pallas kernels, spread(): pl.pallas_call(spread_kernel, grid=(sources,), in_specs=[pl.BlockSpec((1,...  8.67 us
    ppermute x2, waiting for transfers between devices, sum_bands(): values = values + lax.ppermute(values, 'band', pairs)  6.26 us
    pallas_call x1, Pallas kernels, pick(): pl.pallas_call(pick_kernel, grid=(sources,), in_specs=[pl.BlockSpec((1, 1...  5 us
    dot_general x8, matrix products, dot(): return jnp.einsum(subscripts, left, right, precision=HIGHEST)  4.92 us
  transfers between devices with their start and end apart: 4, of which 4 were waited for; matrix products, arithmetic and copies ran while one was open for 5% of the time, Pallas kernels for 0%

profile of v1, /device:TPU:0, one launch (start us, length us, event | category | flops | bytes accessed | tf_op | source)
XLA Modules:
  0.0 134.6 jit_solution(17210027169546781663)
XLA Ops:
  0.6 0.0 copy-start.9
  0.7 0.7 fusion.22
  1.4 0.8 fusion.14
  2.2 0.8 select_reduce_fusion
  3.0 0.7 add_select_fusion.3
  3.7 1.1 bitcast_multiply_fusion
  4.8 1.3 fusion.16
  6.1 0.4 fusion.17
  6.5 0.4 fusion.4
  7.0 0.4 fusion.5
  7.4 0.1 iota_add_fusion
  7.5 1.3 multiply_subtract_fusion.1
  8.8 0.9 pad_maximum_fusion
  9.7 7.3 %all-to-all-start = ((f32[8,25,512]{2,1,0:T(8,128)}), f32[8,25,512]{2,1,0:T(8,128)}, u32[]{:S(2)}, u32[]{:S(2)}) async-start(f32[8,25,512]{2,1,0:T(8,128)} %pad_maximum_fusion), calls=%async_computation | async-start | bytes 1048576 | tf_op jit(solution)/shard_map/all_to_all | solution.py:400
  16.9 0.2 reshape.84
  17.2 0.1 pad.4.refs_1_
  17.2 0.7 constant_dynamic-slice_fusion
  17.9 0.1 fusion.19.refs_2_.refs_3_
  18.0 0.1 fusion.18.refs_4_
  18.1 13.4 %all-to-all-done = f32[8,25,512]{2,1,0:T(8,128)} async-done(((f32[8,25,512]{2,1,0:T(8,128)}), f32[8,25,512]{2,1,0:T(8,128)}, u32[]{:S(2)}, u32[]{:S(2)}) %all-to-all-start) | async-done | bytes 409632 | tf_op jit(solution)/shard_map/all_to_all | solution.py:400
  31.5 0.9 fusion.28
  32.5 0.6 copy.31.cells_ref
  33.2 1.1 slice.33.values_ref
  34.3 8.7 %shard_map.230.refs_0_.refs_1_ = f32[8,24,256]{2,1,0:T(8,128)S(1)} custom-call(s32[8,512,1]{2,1,0:T(8,128)S(1)} %copy.31.cells_ref, f32[8,24,512]{2,1,0:T(8,128)S(1)} %slice.33.values_ref), custom_call_target="tpu_custom_call" | custom-call | tf_op jit(solution)/shard_map/pallas_call | solution.py:145
  43.0 4.2 %shard_map.231 = (f32[8,24,256]{2,1,0:T(8,128)S(1)}, f32[12,96,128]{2,1,0:T(8,128)S(1)}) custom-call(f32[8,24,256]{2,1,0:T(8,128)S(1)} %shard_map.230.refs_0_.refs_1_, f32[12,96,128]{2,1,0:T(8,128)S(1)} %pad.4.refs_1_, f32[96,128]{1,0:T(8,128)S(1)} %copy-done.5, f32[64,192]{1,0:T(8,128)S(1)} %copy-done.2, f32[128,256]{1,0:T(8,128)S(1)} %copy-done.1, ...), custom_call_target="tpu_custom_call" | custom-call | tf_op jit(solution)/shard_map/pallas_call | solution.py:274
  47.2 19.3 %shard_map.232 = (f32[8,24,256]{2,1,0:T(8,128)S(1)}, f32[112,256]{1,0:T(8,128)S(1)}, f32[112,256]{1,0:T(8,128)S(1)}) custom-call(f32[8,24,256]{2,1,0:T(8,128)S(1)} %get-tuple-element.10.refs_0_, f32[8,24,256]{2,1,0:T(8,128)S(1)} %shard_map.230.refs_0_.refs_1_, f32[112,256]{1,0:T(8,128)S(1)} %fusion.19.refs_2_.refs_3_, ...), custom_call_target="tpu_custom_call" | custom-call | tf_op jit(solution)/shard_map/pallas_call | solution.py:359
  66.5 4.2 %shard_map.233.refs_0_ = f32[8,24,256]{2,1,0:T(8,128)S(1)} custom-call(f32[8,24,256]{2,1,0:T(8,128)S(1)} %get-tuple-element.11.refs_0_, f32[12,96,128]{2,1,0:T(8,128)S(1)} %pad.4.refs_1_, f32[96,128]{1,0:T(8,128)S(1)} %copy-done.5, f32[64,192]{1,0:T(8,128)S(1)} %copy-done.2, f32[128,256]{1,0:T(8,128)S(1)} %copy-done.1, f32[256,256]{1,0:T(8,128)S(1)} %copy-done), custom_call_target="tpu_custom_call" | custom-call | tf_op jit(solution)/shard_map/pallas_call | solution.py:274
  70.7 13.5 %shard_map.234 = (f32[8,24,256]{2,1,0:T(8,128)S(1)}, f32[112,256]{1,0:T(8,128)S(1)}, f32[112,256]{1,0:T(8,128)S(1)}) custom-call(f32[8,24,256]{2,1,0:T(8,128)S(1)} %shard_map.233.refs_0_, f32[112,256]{1,0:T(8,128)S(1)} %get-tuple-element.12.refs_1_, f32[112,256]{1,0:T(8,128)S(1)} %get-tuple-element.13.refs_2_, f32[112,256]{1,0:T(8,128)S(1)} %fusion.19.refs_2_.refs_3_, ...), custom_call_target="tpu_custom_call" | custom-call | tf_op jit(solution)/shard_map/pallas_call | solution.py:359
  84.3 4.2 %shard_map.235.refs_0_ = f32[8,24,256]{2,1,0:T(8,128)S(1)} custom-call(f32[8,24,256]{2,1,0:T(8,128)S(1)} %get-tuple-element.14.refs_0_, f32[12,96,128]{2,1,0:T(8,128)S(1)} %pad.4.refs_1_, f32[96,128]{1,0:T(8,128)S(1)} %copy-done.5, f32[64,192]{1,0:T(8,128)S(1)} %copy-done.2, f32[128,256]{1,0:T(8,128)S(1)} %copy-done.1, f32[256,256]{1,0:T(8,128)S(1)} %copy-done), custom_call_target="tpu_custom_call" | custom-call | tf_op jit(solution)/shard_map/pallas_call | solution.py:274
  88.5 14.1 %shard_map.236.refs_0_ = f32[8,24,256]{2,1,0:T(8,128)S(1)} custom-call(f32[8,24,256]{2,1,0:T(8,128)S(1)} %shard_map.235.refs_0_, f32[112,256]{1,0:T(8,128)S(1)} %get-tuple-element.15.refs_1_, f32[112,256]{1,0:T(8,128)S(1)} %get-tuple-element.16.refs_2_, f32[112,256]{1,0:T(8,128)S(1)} %fusion.19.refs_2_.refs_3_, f32[112,256]{1,0:T(8,128)S(1)} %fusion.18.refs_4_, ...), custom_call_target="tpu_custom_call" | custom-call | tf_op jit(solution)/shard_map/pallas_call | solution.py:359
  102.5 2.6 %shard_map.238 = f32[12,96,128]{2,1,0:T(8,128)S(1)} custom-call(f32[8,24,256]{2,1,0:T(8,128)S(1)} %shard_map.236.refs_0_, f32[12,96,128]{2,1,0:T(8,128)S(1)} %pad.4.refs_1_, f32[96,128]{1,0:T(8,128)S(1)} %copy-done.5, f32[64,192]{1,0:T(8,128)S(1)} %copy-done.2, f32[128,256]{1,0:T(8,128)S(1)} %copy-done.1, f32[256,256]{1,0:T(8,128)S(1)} %copy-done), custom_call_target="tpu_custom_call" | custom-call | tf_op jit(solution)/shard_map/pallas_call | solution.py:274
  105.2 5.0 %shard_map.237 = f32[8,24,512]{2,1,0:T(8,128)} custom-call(s32[8,1,512]{2,1,0:T(1,128)S(1)} %get-tuple-element.27.cells_ref, f32[24,2048]{1,0:T(8,128)S(1)} %bitcast.41), custom_call_target="tpu_custom_call" | custom-call | tf_op jit(solution)/shard_map/pallas_call | solution.py:163
  110.2 4.3 %all-to-all-start.1 = ((f32[8,24,512]{2,1,0:T(8,128)}), f32[8,24,512]{2,1,0:T(8,128)S(1)}, u32[]{:S(2)}, u32[]{:S(2)}) async-start(f32[8,24,512]{2,1,0:T(8,128)} %shard_map.237), calls=%async_computation.1 | async-start | bytes 786432 | tf_op jit(solution)/shard_map/all_to_all | solution.py:400
  114.5 0.1 slice_subtract_fusion
  114.5 0.3 reshape.88
  114.9 0.1 collective-permute-start
  115.0 2.0 %collective-permute-done = f32[12,9216]{1,0:T(8,128)S(1)} collective-permute-done((f32[12,9216]{1,0:T(8,128)S(1)}, f32[12,9216]{1,0:T(8,128)S(1)}, u32[]{:S(2)}, u32[]{:S(2)}) %collective-permute-start) | collective-permute-done | bytes 442400 | tf_op jit(solution)/shard_map/ppermute | solution.py:385
  117.0 0.1 add.113
  117.0 1.5 %collective-permute-start.1 = (f32[12,9216]{1,0:T(8,128)S(1)}, f32[12,9216]{1,0:T(8,128)}, u32[]{:S(2)}, u32[]{:S(2)}) collective-permute-start(f32[12,9216]{1,0:T(8,128)S(1)} %add.113), channel_id=1, source_target_pairs={{0,16},{8,24},{16,0},{24,8},{1,17},{9,25},{17,1},{25,9},{2,18},{10... | collective-permute-start | bytes 1327112 | tf_op jit(solution)/shard_map/ppermute | solution.py:385
  118.6 5.1 %all-to-all-done.1 = f32[8,24,512]{2,1,0:T(8,128)S(1)} async-done(((f32[8,24,512]{2,1,0:T(8,128)}), f32[8,24,512]{2,1,0:T(8,128)S(1)}, u32[]{:S(2)}, u32[]{:S(2)}) %all-to-all-start.1) | async-done | bytes 393248 | tf_op jit(solution)/shard_map/all_to_all | solution.py:400
  123.7 1.3 multiply_add_fusion
  125.0 0.6 fusion.30
  125.7 0.6 fusion.29
  126.3 0.6 fusion.1
  126.9 0.6 fusion.3
  127.5 0.8 maximum_bitcast_fusion
  128.3 4.3 %collective-permute-done.1 = f32[12,9216]{1,0:T(8,128)} collective-permute-done((f32[12,9216]{1,0:T(8,128)S(1)}, f32[12,9216]{1,0:T(8,128)}, u32[]{:S(2)}, u32[]{:S(2)}) %collective-permute-start.1) | collective-permute-done | bytes 442400 | tf_op jit(solution)/shard_map/ppermute | solution.py:385
  132.6 2.0 %fusion.6 = f32[12,9216]{1,0:T(8,128)} fusion(f32[12,9216]{1,0:T(8,128)S(1)} %copy-done.6, f32[12,9216]{1,0:T(8,128)S(1)} %add.113, f32[12,9216]{1,0:T(8,128)} %collective-permute-done.1), kind=kLoop, calls=%fused_computation.11 | loop fusion | flops 774144 | bytes 1769472 | tf_op jit(solution)/shard_map/add | solution.py:462
  (32 shorter events, 0.2 us)
Async XLA Ops:
  0.6 6.3 %copy-start.7 = (f32[128,96]{1,0:T(8,128)S(1)}, f32[128,96]{1,0:T(8,128)}, u32[]{:S(2)}) copy-start(f32[128,96]{1,0:T(8,128)} %constant.96.clone) | copy-start | bytes 147460
  0.6 5.4 %copy-start.9 = (f32[128,96]{1,0:T(8,128)S(1)}, f32[128,96]{1,0:T(8,128)}, u32[]{:S(2)}) copy-start(f32[128,96]{1,0:T(8,128)} %constant.95.clone) | copy-start | bytes 147460
  7.0 10.0 %copy-start.6 = (f32[12,9216]{1,0:T(8,128)S(1)}, f32[12,9216]{1,0:T(8,128)}, u32[]{:S(2)}) copy-start(f32[12,9216]{1,0:T(8,128)} %param.24) | copy-start | bytes 1327108
  8.8 9.1 %copy-start.12 = (s32[112]{0:T(128)S(1)}, s32[112]{0:T(128)}, u32[]{:S(2)}) copy-start(s32[112]{0:T(128)} %constant.111) | copy-start | bytes 1348
  9.7 21.8 %all-to-all-start = ((f32[8,25,512]{2,1,0:T(8,128)}), f32[8,25,512]{2,1,0:T(8,128)}, u32[]{:S(2)}, u32[]{:S(2)}) async-start(f32[8,25,512]{2,1,0:T(8,128)} %pad_maximum_fusion), calls=%async_computation | async-start | bytes 1048576 | tf_op jit(solution)/shard_map/all_to_all | solution.py:400
  33.1 9.8 %copy-start = (f32[256,256]{1,0:T(8,128)S(1)}, f32[256,256]{1,0:T(8,128)}, u32[]{:S(2)}) copy-start(f32[256,256]{1,0:T(8,128)} %constant.103.clone.refs_5_) | copy-start | bytes 786436
  33.1 9.8 %copy-start.1 = (f32[128,256]{1,0:T(8,128)S(1)}, f32[128,256]{1,0:T(8,128)}, u32[]{:S(2)}) copy-start(f32[128,256]{1,0:T(8,128)} %constant.102.clone.refs_4_) | copy-start | bytes 393220
  33.1 9.8 %copy-start.2 = (f32[64,192]{1,0:T(8,128)S(1)}, f32[64,192]{1,0:T(8,128)}, u32[]{:S(2)}) copy-start(f32[64,192]{1,0:T(8,128)} %constant.101.clone.refs_3_) | copy-start | bytes 147460
  33.1 9.8 %copy-start.5 = (f32[96,128]{1,0:T(8,128)S(1)}, f32[96,128]{1,0:T(8,128)}, u32[]{:S(2)}) copy-start(f32[96,128]{1,0:T(8,128)} %constant.100.clone.refs_2_) | copy-start | bytes 147460
  34.2 12.9 %copy-start.3 = (f32[112,192]{1,0:T(8,128)S(1)}, f32[112,192]{1,0:T(8,128)}, u32[]{:S(2)}) copy-start(f32[112,192]{1,0:T(8,128)} %constant.105.clone.refs_6_) | copy-start | bytes 258052
  34.2 12.9 %copy-start.4 = (f32[192,112]{1,0:T(8,128)S(1)}, f32[192,112]{1,0:T(8,128)}, u32[]{:S(2)}) copy-start(f32[192,112]{1,0:T(8,128)} %constant.104.clone.refs_5_) | copy-start | bytes 258052
  110.2 13.5 %all-to-all-start.1 = ((f32[8,24,512]{2,1,0:T(8,128)}), f32[8,24,512]{2,1,0:T(8,128)S(1)}, u32[]{:S(2)}, u32[]{:S(2)}) async-start(f32[8,24,512]{2,1,0:T(8,128)} %shard_map.237), calls=%async_computation.1 | async-start | bytes 786432 | tf_op jit(solution)/shard_map/all_to_all | solution.py:400
  114.5 10.5 %copy-start.10 = (f32[128,96]{1,0:T(8,128)S(1)}, f32[128,96]{1,0:T(8,128)}, u32[]{:S(2)}) copy-start(f32[128,96]{1,0:T(8,128)} %constant.95.clone) | copy-start | bytes 147460
  114.9 11.4 %copy-start.8 = (f32[128,96]{1,0:T(8,128)S(1)}, f32[128,96]{1,0:T(8,128)}, u32[]{:S(2)}) copy-start(f32[128,96]{1,0:T(8,128)} %constant.96.clone) | copy-start | bytes 147460
  114.9 11.4 %copy-start.11 = (s32[512]{0:T(512)S(1)}, s32[512]{0:T(512)}, u32[]{:S(2)}) copy-start(s32[512]{0:T(512)} %param.26) | copy-start | bytes 6148
  114.9 2.1 %collective-permute-start = (f32[12,9216]{1,0:T(8,128)S(1)}, f32[12,9216]{1,0:T(8,128)S(1)}, u32[]{:S(2)}, u32[]{:S(2)}) collective-permute-start(f32[12,9216]{1,0:T(8,128)S(1)} %reshape.88), channel_id=1, source_target_pairs={{0,8},{8,0},{16,24},{24,16},{1,9},{9,1},{17,25},{25,17},{2,10},{10... | collective-permute-start | bytes 1327112 | tf_op jit(solution)/shard_map/ppermute | solution.py:385
  117.0 15.5 %collective-permute-start.1 = (f32[12,9216]{1,0:T(8,128)S(1)}, f32[12,9216]{1,0:T(8,128)}, u32[]{:S(2)}, u32[]{:S(2)}) collective-permute-start(f32[12,9216]{1,0:T(8,128)S(1)} %add.113), channel_id=1, source_target_pairs={{0,16},{8,24},{16,0},{24,8},{1,17},{9,25},{17,1},{25,9},{2,18},{10... | collective-permute-start | bytes 1327112 | tf_op jit(solution)/shard_map/ppermute | solution.py:385

commit v2 on v1

--- a/solution.py
+++ b/solution.py
@@ -301,10 +301,7 @@
     return copies
 
 
-def height_kernel(count, factor, opening, last, *refs):
-    spectrum_ref, term_ref, total_ref, kinetic_ref, inside_ref, table_ref, turned_ref = refs[:7]
-    outs, scratch = refs[7 : 8 if last else 10], refs[8 if last else 10 :]
-    landed, sent, final, flat, send_sem, recv_sem, send_later, recv_later = scratch[:8]
+def greet(count):
     me = lax.axis_index("plane")
     band = lax.axis_index("band")
     barrier = pltpu.get_barrier_semaphore()
@@ -316,6 +313,36 @@
             device_id_type=pl.DeviceIdType.MESH,
         )
     pl.semaphore_wait(barrier, count - 1)
+
+
+def swap_kernel(count, sent_ref, out_ref, landed, send_sem, recv_sem):
+    greet(count)
+    for copy in trade(count, sent_ref, landed, send_sem, recv_sem):
+        copy.wait()
+    out_ref[...] = landed[...]
+
+
+def swap(values, collective_id):
+    count = values.shape[0]
+    whole = pl.BlockSpec(memory_space=pltpu.VMEM)
+    return pl.pallas_call(
+        functools.partial(swap_kernel, count),
+        in_specs=[whole],
+        out_specs=whole,
+        out_shape=jax.ShapeDtypeStruct(values.shape, jnp.float32),
+        scratch_shapes=[pltpu.VMEM(values.shape, jnp.float32)]
+        + [pltpu.SemaphoreType.DMA((count - 1,))] * 2,
+        compiler_params=pltpu.CompilerParams(
+            vmem_limit_bytes=40 << 20, collective_id=collective_id, has_side_effects=True
+        ),
+    )(values)
+
+
+def height_kernel(count, factor, opening, last, *refs):
+    spectrum_ref, term_ref, total_ref, kinetic_ref, inside_ref, table_ref, turned_ref = refs[:7]
+    outs, scratch = refs[7 : 8 if last else 10], refs[8 if last else 10 :]
+    landed, sent, final, flat, send_sem, recv_sem, send_later, recv_later = scratch[:8]
+    greet(count)
     copies = trade(count, spectrum_ref, landed, send_sem, recv_sem)
     if opening:
         origin, origin_send, origin_recv = scratch[8:]
@@ -419,7 +446,7 @@
         ],
         axis=1,
     )
-    arrived = exchange(packed)
+    arrived = swap(packed, 4)
     cells = arrived[:, 2 * planes, :].astype(jnp.int32)
     start = spread(cells, arrived[:, : 2 * planes, :], device_list, lanes)
 

time: 135 us -> 133 us (0.985)
  Pallas kernels: 75.8 us -> 94.5 us
  waiting for transfers between devices: 24.8 us -> 11.3 us
  starting transfers between devices: 13.1 us -> 6.25 us
  other arithmetic: 11.7 us -> 10 us
    all_to_all x2 -> x1, waiting for transfers between devices: 18.5 us -> 2.66 us  [exchange(): lax.all_to_all(values, 'plane', split_axis=0, concat_axis=0, tiled=True)]
    pallas_call x0 -> x1, Pallas kernels: none -> 14.6 us  [swap(): pl.pallas_call(functools.partial(swap_kernel, count), in_specs=[whole], o...]
    all_to_all x2 -> x1, starting transfers between devices: 11.5 us -> 4.58 us  [exchange(): lax.all_to_all(values, 'plane', split_axis=0, concat_axis=0, tiled=True)]
    pallas_call x3, Pallas kernels: 46.9 us -> 51.3 us  [height_step(): pl.pallas_call(functools.partial(height_kernel, count, TIMESTEP / power,...]
    ppermute x2, waiting for transfers between devices: 6.26 us -> 8.63 us  [sum_bands(): values = values + lax.ppermute(values, 'band', pairs)]
    reshape x1, local copies, waits for them, and re-layouts: 0.2 us -> 2.12 us  [shards(): potential.reshape(planes, NG, NG)]
  transfers between devices with their start and end apart: 4 -> 3, of which waited for: 4 -> 3; matrix products, arithmetic and copies ran while one was open for 5% -> 4% of each run, Pallas kernels for 0% -> 2%
where the time goes in v2:
time: 133 us; the launch traced here: 132 us
  Pallas kernels  94.5 us (71%)
  waiting for transfers between devices  11.3 us (8%)
  other arithmetic  10 us (8%)
  starting transfers between devices  6.25 us (5%)
  matrix products  4.92 us (4%)
  local copies, waits for them, and re-layouts  4.08 us (3%)
    pallas_call x3, Pallas kernels, height_step(): pl.pallas_call(functools.partial(height_kernel, count, TIMESTEP / power,...  51.3 us
    pallas_call x4, Pallas kernels, plane_step(): pl.pallas_call(kernel, in_specs=[whole] * 6, out_specs=[whole] * len(shap...  14.9 us
    pallas_call x1, Pallas kernels, swap(): pl.pallas_call(functools.partial(swap_kernel, count), in_specs=[whole], o...  14.6 us
    pallas_call x1, Pallas kernels, spread(): pl.pallas_call(spread_kernel, grid=(sources,), in_specs=[pl.BlockSpec((1,...  8.67 us
    ppermute x2, waiting for transfers between devices, sum_bands(): values = values + lax.ppermute(values, 'band', pairs)  8.63 us
    pallas_call x1, Pallas kernels, pick(): pl.pallas_call(pick_kernel, grid=(sources,), in_specs=[pl.BlockSpec((1, 1...  5 us
    dot_general x8, matrix products, dot(): return jnp.einsum(subscripts, left, right, precision=HIGHEST)  4.92 us
    all_to_all x1, starting transfers between devices, exchange(): lax.all_to_all(values, 'plane', split_axis=0, concat_axis=0, tiled=True)  4.58 us
  transfers between devices with their start and end apart: 3, of which 3 were waited for; matrix products, arithmetic and copies ran while one was open for 4% of the time, Pallas kernels for 2%

profile of v2, /device:TPU:0, one launch (start us, length us, event | category | flops | bytes accessed | tf_op | source)
XLA Modules:
  0.0 132.1 jit_solution(4461151590328114176)
XLA Ops:
  0.6 0.0 copy-start.8
  0.6 0.0 copy-start.9
  0.7 0.7 fusion.22
  1.4 0.8 fusion.14
  2.2 0.8 select_reduce_fusion
  3.0 0.7 add_select_fusion.3
  3.7 1.1 bitcast_multiply_fusion
  4.8 1.3 fusion.16
  6.1 0.4 fusion.17
  6.5 0.4 fusion.4
  7.0 0.4 fusion.5
  7.4 0.1 iota_add_fusion
  7.5 1.3 multiply_subtract_fusion.1
  8.8 0.1 pad_maximum_fusion.sent_ref
  8.9 14.6 %shard_map.230 = f32[8,25,512]{2,1,0:T(8,128)S(1)} custom-call(f32[8,25,512]{2,1,0:T(8,128)S(1)} %pad_maximum_fusion.sent_ref), custom_call_target="tpu_custom_call" | custom-call | tf_op jit(solution)/shard_map/pallas_call | solution.py:328
  23.6 0.7 constant_dynamic-slice_fusion
  24.3 0.1 fusion.19.refs_2_.refs_3_
  24.4 0.1 fusion.18.refs_4_
  24.5 0.6 copy.31.cells_ref
  25.1 2.1 %reshape.84 = f32[12,96,96]{2,1,0:T(8,128)} reshape(f32[12,9216]{1,0:T(8,128)} %param.24) | data formatting | bytes 884736 | tf_op jit(solution)/shard_map/reshape | solution.py:453
  27.2 0.0 copy-start.5
  27.2 0.0 copy-start.3
  27.3 0.0 copy-start.4
  27.3 8.7 %shard_map.231.refs_0_.refs_1_ = f32[8,24,256]{2,1,0:T(8,128)S(1)} custom-call(s32[8,512,1]{2,1,0:T(8,128)S(1)} %copy.31.cells_ref, f32[8,24,512]{2,1,0:T(8,128)S(1)} %slice.26.values_ref), custom_call_target="tpu_custom_call" | custom-call | tf_op jit(solution)/shard_map/pallas_call | solution.py:145
  36.1 4.2 %shard_map.232 = (f32[8,24,256]{2,1,0:T(8,128)S(1)}, f32[12,96,128]{2,1,0:T(8,128)S(1)}) custom-call(f32[8,24,256]{2,1,0:T(8,128)S(1)} %shard_map.231.refs_0_.refs_1_, f32[12,96,128]{2,1,0:T(8,128)S(1)} %pad.4.refs_1_, f32[96,128]{1,0:T(8,128)S(1)} %copy-done.5, f32[64,192]{1,0:T(8,128)S(1)} %copy-done.2, f32[128,256]{1,0:T(8,128)S(1)} %copy-done.1, ...), custom_call_target="tpu_custom_call" | custom-call | tf_op jit(solution)/shard_map/pallas_call | solution.py:274
  40.3 22.6 %shard_map.233 = (f32[8,24,256]{2,1,0:T(8,128)S(1)}, f32[112,256]{1,0:T(8,128)S(1)}, f32[112,256]{1,0:T(8,128)S(1)}) custom-call(f32[8,24,256]{2,1,0:T(8,128)S(1)} %get-tuple-element.10.refs_0_, f32[8,24,256]{2,1,0:T(8,128)S(1)} %shard_map.231.refs_0_.refs_1_, f32[112,256]{1,0:T(8,128)S(1)} %fusion.19.refs_2_.refs_3_, ...), custom_call_target="tpu_custom_call" | custom-call | tf_op jit(solution)/shard_map/pallas_call | solution.py:386
  62.8 4.2 %shard_map.234.refs_0_ = f32[8,24,256]{2,1,0:T(8,128)S(1)} custom-call(f32[8,24,256]{2,1,0:T(8,128)S(1)} %get-tuple-element.11.refs_0_, f32[12,96,128]{2,1,0:T(8,128)S(1)} %pad.4.refs_1_, f32[96,128]{1,0:T(8,128)S(1)} %copy-done.5, f32[64,192]{1,0:T(8,128)S(1)} %copy-done.2, f32[128,256]{1,0:T(8,128)S(1)} %copy-done.1, f32[256,256]{1,0:T(8,128)S(1)} %copy-done), custom_call_target="tpu_custom_call" | custom-call | tf_op jit(solution)/shard_map/pallas_call | solution.py:274
  67.0 15.5 %shard_map.235 = (f32[8,24,256]{2,1,0:T(8,128)S(1)}, f32[112,256]{1,0:T(8,128)S(1)}, f32[112,256]{1,0:T(8,128)S(1)}) custom-call(f32[8,24,256]{2,1,0:T(8,128)S(1)} %shard_map.234.refs_0_, f32[112,256]{1,0:T(8,128)S(1)} %get-tuple-element.12.refs_1_, f32[112,256]{1,0:T(8,128)S(1)} %get-tuple-element.13.refs_2_, f32[112,256]{1,0:T(8,128)S(1)} %fusion.19.refs_2_.refs_3_, ...), custom_call_target="tpu_custom_call" | custom-call | tf_op jit(solution)/shard_map/pallas_call | solution.py:386
  82.5 4.2 %shard_map.236.refs_0_ = f32[8,24,256]{2,1,0:T(8,128)S(1)} custom-call(f32[8,24,256]{2,1,0:T(8,128)S(1)} %get-tuple-element.14.refs_0_, f32[12,96,128]{2,1,0:T(8,128)S(1)} %pad.4.refs_1_, f32[96,128]{1,0:T(8,128)S(1)} %copy-done.5, f32[64,192]{1,0:T(8,128)S(1)} %copy-done.2, f32[128,256]{1,0:T(8,128)S(1)} %copy-done.1, f32[256,256]{1,0:T(8,128)S(1)} %copy-done), custom_call_target="tpu_custom_call" | custom-call | tf_op jit(solution)/shard_map/pallas_call | solution.py:274
  86.7 13.3 %shard_map.237.refs_0_ = f32[8,24,256]{2,1,0:T(8,128)S(1)} custom-call(f32[8,24,256]{2,1,0:T(8,128)S(1)} %shard_map.236.refs_0_, f32[112,256]{1,0:T(8,128)S(1)} %get-tuple-element.15.refs_1_, f32[112,256]{1,0:T(8,128)S(1)} %get-tuple-element.16.refs_2_, f32[112,256]{1,0:T(8,128)S(1)} %fusion.19.refs_2_.refs_3_, f32[112,256]{1,0:T(8,128)S(1)} %fusion.18.refs_4_, ...), custom_call_target="tpu_custom_call" | custom-call | tf_op jit(solution)/shard_map/pallas_call | solution.py:386
  100.0 5.0 %shard_map.238 = f32[8,24,512]{2,1,0:T(8,128)} custom-call(s32[8,1,512]{2,1,0:T(1,128)S(1)} %get-tuple-element.27.cells_ref, f32[24,2048]{1,0:T(8,128)S(1)} %bitcast.41), custom_call_target="tpu_custom_call" | custom-call | tf_op jit(solution)/shard_map/pallas_call | solution.py:163
  105.0 4.6 %all-to-all-start = ((f32[8,24,512]{2,1,0:T(8,128)}), f32[8,24,512]{2,1,0:T(8,128)S(1)}, u32[]{:S(2)}, u32[]{:S(2)}) async-start(f32[8,24,512]{2,1,0:T(8,128)} %shard_map.238), calls=%async_computation | async-start | bytes 786432 | tf_op jit(solution)/shard_map/all_to_all | solution.py:427
  109.6 2.4 %shard_map.239 = f32[12,96,128]{2,1,0:T(8,128)S(1)} custom-call(f32[8,24,256]{2,1,0:T(8,128)S(1)} %shard_map.237.refs_0_, f32[12,96,128]{2,1,0:T(8,128)S(1)} %pad.4.refs_1_, f32[96,128]{1,0:T(8,128)S(1)} %copy-done.5, f32[64,192]{1,0:T(8,128)S(1)} %copy-done.2, f32[128,256]{1,0:T(8,128)S(1)} %copy-done.1, f32[256,256]{1,0:T(8,128)S(1)} %copy-done), custom_call_target="tpu_custom_call" | custom-call | tf_op jit(solution)/shard_map/pallas_call | solution.py:274
  112.0 0.1 slice_subtract_fusion
  112.1 0.3 reshape.88
  112.4 0.1 collective-permute-start
  112.5 2.0 %collective-permute-done = f32[12,9216]{1,0:T(8,128)S(1)} collective-permute-done((f32[12,9216]{1,0:T(8,128)S(1)}, f32[12,9216]{1,0:T(8,128)S(1)}, u32[]{:S(2)}, u32[]{:S(2)}) %collective-permute-start) | collective-permute-done | bytes 442400 | tf_op jit(solution)/shard_map/ppermute | solution.py:412
  114.5 0.1 add.113
  114.5 1.6 %collective-permute-start.1 = (f32[12,9216]{1,0:T(8,128)S(1)}, f32[12,9216]{1,0:T(8,128)}, u32[]{:S(2)}, u32[]{:S(2)}) collective-permute-start(f32[12,9216]{1,0:T(8,128)S(1)} %add.113), channel_id=1, source_target_pairs={{0,16},{8,24},{16,0},{24,8},{1,17},{9,25},{17,1},{25,9},{2,18},{10... | collective-permute-start | bytes 1327112 | tf_op jit(solution)/shard_map/ppermute | solution.py:412
  116.1 2.7 %all-to-all-done = f32[8,24,512]{2,1,0:T(8,128)S(1)} async-done(((f32[8,24,512]{2,1,0:T(8,128)}), f32[8,24,512]{2,1,0:T(8,128)S(1)}, u32[]{:S(2)}, u32[]{:S(2)}) %all-to-all-start) | async-done | bytes 393248 | tf_op jit(solution)/shard_map/all_to_all | solution.py:427
  118.8 1.3 multiply_add_fusion
  120.2 0.6 fusion.30
  120.8 0.6 fusion.29
  121.4 0.6 fusion.1
  122.0 0.6 fusion.3
  122.6 0.8 maximum_bitcast_fusion
  123.4 6.6 %collective-permute-done.1 = f32[12,9216]{1,0:T(8,128)} collective-permute-done((f32[12,9216]{1,0:T(8,128)S(1)}, f32[12,9216]{1,0:T(8,128)}, u32[]{:S(2)}, u32[]{:S(2)}) %collective-permute-start.1) | collective-permute-done | bytes 442400 | tf_op jit(solution)/shard_map/ppermute | solution.py:412
  130.1 2.0 %fusion.6 = f32[12,9216]{1,0:T(8,128)} fusion(f32[12,9216]{1,0:T(8,128)S(1)} %copy-done.7, f32[12,9216]{1,0:T(8,128)S(1)} %add.113, f32[12,9216]{1,0:T(8,128)} %collective-permute-done.1), kind=kLoop, calls=%fused_computation.11 | loop fusion | flops 774144 | bytes 1769472 | tf_op jit(solution)/shard_map/add | solution.py:489
  (29 shorter events, 0.3 us)
Async XLA Ops:
  0.6 6.3 %copy-start.8 = (f32[128,96]{1,0:T(8,128)S(1)}, f32[128,96]{1,0:T(8,128)}, u32[]{:S(2)}) copy-start(f32[128,96]{1,0:T(8,128)} %constant.96.clone) | copy-start | bytes 147460
  0.6 5.4 %copy-start.9 = (f32[128,96]{1,0:T(8,128)S(1)}, f32[128,96]{1,0:T(8,128)}, u32[]{:S(2)}) copy-start(f32[128,96]{1,0:T(8,128)} %constant.95.clone) | copy-start | bytes 147460
  7.4 16.9 %copy-start.11 = (s32[112]{0:T(128)S(1)}, s32[112]{0:T(128)}, u32[]{:S(2)}) copy-start(s32[112]{0:T(128)} %constant.111) | copy-start | bytes 1348
  27.2 8.7 %copy-start.6 = (f32[12,96,96]{2,1,0:T(8,128)S(1)}, f32[12,96,96]{2,1,0:T(8,128)}, u32[]{:S(2)}) copy-start(f32[12,96,96]{2,1,0:T(8,128)} %reshape.84) | copy-start | bytes 1327108
  27.2 8.8 %copy-start = (f32[256,256]{1,0:T(8,128)S(1)}, f32[256,256]{1,0:T(8,128)}, u32[]{:S(2)}) copy-start(f32[256,256]{1,0:T(8,128)} %constant.103.clone.refs_5_) | copy-start | bytes 786436
  27.2 8.8 %copy-start.1 = (f32[128,256]{1,0:T(8,128)S(1)}, f32[128,256]{1,0:T(8,128)}, u32[]{:S(2)}) copy-start(f32[128,256]{1,0:T(8,128)} %constant.102.clone.refs_4_) | copy-start | bytes 393220
  27.2 8.8 %copy-start.2 = (f32[64,192]{1,0:T(8,128)S(1)}, f32[64,192]{1,0:T(8,128)}, u32[]{:S(2)}) copy-start(f32[64,192]{1,0:T(8,128)} %constant.101.clone.refs_3_) | copy-start | bytes 147460
  27.2 8.8 %copy-start.5 = (f32[96,128]{1,0:T(8,128)S(1)}, f32[96,128]{1,0:T(8,128)}, u32[]{:S(2)}) copy-start(f32[96,128]{1,0:T(8,128)} %constant.100.clone.refs_2_) | copy-start | bytes 147460
  27.2 13.0 %copy-start.3 = (f32[112,192]{1,0:T(8,128)S(1)}, f32[112,192]{1,0:T(8,128)}, u32[]{:S(2)}) copy-start(f32[112,192]{1,0:T(8,128)} %constant.105.clone.refs_6_) | copy-start | bytes 258052
  27.3 13.0 %copy-start.4 = (f32[192,112]{1,0:T(8,128)S(1)}, f32[192,112]{1,0:T(8,128)}, u32[]{:S(2)}) copy-start(f32[192,112]{1,0:T(8,128)} %constant.104.clone.refs_5_) | copy-start | bytes 258052
  105.0 13.8 %all-to-all-start = ((f32[8,24,512]{2,1,0:T(8,128)}), f32[8,24,512]{2,1,0:T(8,128)S(1)}, u32[]{:S(2)}, u32[]{:S(2)}) async-start(f32[8,24,512]{2,1,0:T(8,128)} %shard_map.238), calls=%async_computation | async-start | bytes 786432 | tf_op jit(solution)/shard_map/all_to_all | solution.py:427
  112.4 9.0 %copy-start.10 = (s32[512]{0:T(512)S(1)}, s32[512]{0:T(512)}, u32[]{:S(2)}) copy-start(s32[512]{0:T(512)} %param.26) | copy-start | bytes 6148
  112.4 2.1 %collective-permute-start = (f32[12,9216]{1,0:T(8,128)S(1)}, f32[12,9216]{1,0:T(8,128)S(1)}, u32[]{:S(2)}, u32[]{:S(2)}) collective-permute-start(f32[12,9216]{1,0:T(8,128)S(1)} %reshape.88), channel_id=1, source_target_pairs={{0,8},{8,0},{16,24},{24,16},{1,9},{9,1},{17,25},{25,17},{2,10},{10... | collective-permute-start | bytes 1327112 | tf_op jit(solution)/shard_map/ppermute | solution.py:412
  114.5 15.5 %collective-permute-start.1 = (f32[12,9216]{1,0:T(8,128)S(1)}, f32[12,9216]{1,0:T(8,128)}, u32[]{:S(2)}, u32[]{:S(2)}) collective-permute-start(f32[12,9216]{1,0:T(8,128)S(1)} %add.113), channel_id=1, source_target_pairs={{0,16},{8,24},{16,0},{24,8},{1,17},{9,25},{17,1},{25,9},{2,18},{10... | collective-permute-start | bytes 1327112 | tf_op jit(solution)/shard_map/ppermute | solution.py:412
  120.1 9.9 %copy-start.7 = (f32[12,9216]{1,0:T(8,128)S(1)}, f32[12,9216]{1,0:T(8,128)}, u32[]{:S(2)}) copy-start(f32[12,9216]{1,0:T(8,128)} %param.24) | copy-start | bytes 1327108

commit v3 on v2

--- a/solution.py
+++ b/solution.py
@@ -471,6 +471,7 @@
     (spectrum,) = plane_step(layout, arrived, local, tables, False, True)
     (final,) = height_step(3, spectrum, term, total, kinetic, inside, table)
     (after,) = plane_step(layout, final, local, tables, True, False)
+    final, after = lax.optimization_barrier((final, after))
     flat = final.transpose(1, 0, 2).reshape(2 * planes, device_list * lanes)
     home = exchange(pick(cells, flat))
     real, imag = home[:, :planes], home[:, planes:]

time: 133 us -> 131 us (0.985)
    ppermute x2, waiting for transfers between devices: 8.63 us -> 6.14 us  [sum_bands(): values = values + lax.ppermute(values, 'band', pairs)]
    all_to_all x1, waiting for transfers between devices: 2.66 us -> 5.01 us  [exchange(): lax.all_to_all(values, 'plane', split_axis=0, concat_axis=0, tiled=True)]
  transfers between devices with their start and end apart: 3 -> 3, of which waited for: 3 -> 3; matrix products, arithmetic and copies ran while one was open for 4% -> 4% of each run, Pallas kernels for 2% -> 0%
where the time goes in v3:
time: 131 us; the launch traced here: 130 us
  Pallas kernels  94.8 us (72%)
  waiting for transfers between devices  11.2 us (9%)
  other arithmetic  8.95 us (7%)
  starting transfers between devices  6.16 us (5%)
  matrix products  4.92 us (4%)
  local copies, waits for them, and re-layouts  3.27 us (2%)
    pallas_call x3, Pallas kernels, height_step(): pl.pallas_call(functools.partial(height_kernel, count, TIMESTEP / power,...  51.4 us
    pallas_call x4, Pallas kernels, plane_step(): pl.pallas_call(kernel, in_specs=[whole] * 6, out_specs=[whole] * len(shap...  15.2 us
    pallas_call x1, Pallas kernels, swap(): pl.pallas_call(functools.partial(swap_kernel, count), in_specs=[whole], o...  14.6 us
    pallas_call x1, Pallas kernels, spread(): pl.pallas_call(spread_kernel, grid=(sources,), in_specs=[pl.BlockSpec((1,...  8.67 us
    ppermute x2, waiting for transfers between devices, sum_bands(): values = values + lax.ppermute(values, 'band', pairs)  6.14 us
    all_to_all x1, waiting for transfers between devices, exchange(): lax.all_to_all(values, 'plane', split_axis=0, concat_axis=0, tiled=True)  5.01 us
    pallas_call x1, Pallas kernels, pick(): pl.pallas_call(pick_kernel, grid=(sources,), in_specs=[pl.BlockSpec((1, 1...  5 us
    dot_general x8, matrix products, dot(): return jnp.einsum(subscripts, left, right, precision=HIGHEST)  4.92 us
  transfers between devices with their start and end apart: 3, of which 3 were waited for; matrix products, arithmetic and copies ran while one was open for 4% of the time, Pallas kernels for 0%

profile of v3, /device:TPU:0, one launch (start us, length us, event | category | flops | bytes accessed | tf_op | source)
XLA Modules:
  0.0 130.4 jit_solution(3363979927695512390)
XLA Ops:
  0.6 0.0 copy-start.7
  0.6 0.0 copy-start.9
  0.7 0.7 fusion.22
  1.4 0.8 fusion.14
  2.2 0.8 select_reduce_fusion
  3.0 0.7 add_select_fusion.3
  3.7 1.1 bitcast_multiply_fusion
  4.8 1.3 fusion.16
  6.1 0.4 fusion.17
  6.5 0.4 fusion.4
  7.0 0.4 fusion.5
  7.4 0.0 copy-start.12
  7.4 0.1 iota_add_fusion
  7.5 1.3 multiply_subtract_fusion.1
  8.8 0.1 pad_maximum_fusion.sent_ref
  8.9 14.6 %shard_map.230 = f32[8,25,512]{2,1,0:T(8,128)S(1)} custom-call(f32[8,25,512]{2,1,0:T(8,128)S(1)} %pad_maximum_fusion.sent_ref), custom_call_target="tpu_custom_call" | custom-call | tf_op jit(solution)/shard_map/pallas_call | solution.py:328
  23.6 0.7 constant_dynamic-slice_fusion
  24.3 0.1 fusion.19.refs_2_.refs_3_
  24.4 0.1 fusion.18.refs_4_
  24.5 0.6 copy.31.cells_ref
  25.1 1.3 reshape.84
  26.4 0.0 copy-start
  26.4 0.0 copy-start.1
  26.5 8.7 %shard_map.231.refs_0_.refs_1_ = f32[8,24,256]{2,1,0:T(8,128)S(1)} custom-call(s32[8,512,1]{2,1,0:T(8,128)S(1)} %copy.31.cells_ref, f32[8,24,512]{2,1,0:T(8,128)S(1)} %slice.26.values_ref), custom_call_target="tpu_custom_call" | custom-call | tf_op jit(solution)/shard_map/pallas_call | solution.py:145
  35.3 4.2 %shard_map.232 = (f32[8,24,256]{2,1,0:T(8,128)S(1)}, f32[12,96,128]{2,1,0:T(8,128)S(1)}) custom-call(f32[8,24,256]{2,1,0:T(8,128)S(1)} %shard_map.231.refs_0_.refs_1_, f32[12,96,128]{2,1,0:T(8,128)S(1)} %pad.4.refs_1_, f32[96,128]{1,0:T(8,128)S(1)} %copy-done.5, f32[64,192]{1,0:T(8,128)S(1)} %copy-done.2, f32[128,256]{1,0:T(8,128)S(1)} %copy-done.1, ...), custom_call_target="tpu_custom_call" | custom-call | tf_op jit(solution)/shard_map/pallas_call | solution.py:274
  39.5 22.6 %shard_map.233 = (f32[8,24,256]{2,1,0:T(8,128)S(1)}, f32[112,256]{1,0:T(8,128)S(1)}, f32[112,256]{1,0:T(8,128)S(1)}) custom-call(f32[8,24,256]{2,1,0:T(8,128)S(1)} %get-tuple-element.12.refs_0_, f32[8,24,256]{2,1,0:T(8,128)S(1)} %shard_map.231.refs_0_.refs_1_, f32[112,256]{1,0:T(8,128)S(1)} %fusion.19.refs_2_.refs_3_, ...), custom_call_target="tpu_custom_call" | custom-call | tf_op jit(solution)/shard_map/pallas_call | solution.py:386
  62.0 4.2 %shard_map.234.refs_0_ = f32[8,24,256]{2,1,0:T(8,128)S(1)} custom-call(f32[8,24,256]{2,1,0:T(8,128)S(1)} %get-tuple-element.13.refs_0_, f32[12,96,128]{2,1,0:T(8,128)S(1)} %pad.4.refs_1_, f32[96,128]{1,0:T(8,128)S(1)} %copy-done.5, f32[64,192]{1,0:T(8,128)S(1)} %copy-done.2, f32[128,256]{1,0:T(8,128)S(1)} %copy-done.1, f32[256,256]{1,0:T(8,128)S(1)} %copy-done), custom_call_target="tpu_custom_call" | custom-call | tf_op jit(solution)/shard_map/pallas_call | solution.py:274
  66.2 15.5 %shard_map.235 = (f32[8,24,256]{2,1,0:T(8,128)S(1)}, f32[112,256]{1,0:T(8,128)S(1)}, f32[112,256]{1,0:T(8,128)S(1)}) custom-call(f32[8,24,256]{2,1,0:T(8,128)S(1)} %shard_map.234.refs_0_, f32[112,256]{1,0:T(8,128)S(1)} %get-tuple-element.14.refs_1_, f32[112,256]{1,0:T(8,128)S(1)} %get-tuple-element.15.refs_2_, f32[112,256]{1,0:T(8,128)S(1)} %fusion.19.refs_2_.refs_3_, ...), custom_call_target="tpu_custom_call" | custom-call | tf_op jit(solution)/shard_map/pallas_call | solution.py:386
  81.7 4.2 %shard_map.236.refs_0_ = f32[8,24,256]{2,1,0:T(8,128)S(1)} custom-call(f32[8,24,256]{2,1,0:T(8,128)S(1)} %get-tuple-element.16.refs_0_, f32[12,96,128]{2,1,0:T(8,128)S(1)} %pad.4.refs_1_, f32[96,128]{1,0:T(8,128)S(1)} %copy-done.5, f32[64,192]{1,0:T(8,128)S(1)} %copy-done.2, f32[128,256]{1,0:T(8,128)S(1)} %copy-done.1, f32[256,256]{1,0:T(8,128)S(1)} %copy-done), custom_call_target="tpu_custom_call" | custom-call | tf_op jit(solution)/shard_map/pallas_call | solution.py:274
  85.9 13.4 %shard_map.237.refs_0_ = f32[8,24,256]{2,1,0:T(8,128)S(1)} custom-call(f32[8,24,256]{2,1,0:T(8,128)S(1)} %shard_map.236.refs_0_, f32[112,256]{1,0:T(8,128)S(1)} %get-tuple-element.17.refs_1_, f32[112,256]{1,0:T(8,128)S(1)} %get-tuple-element.18.refs_2_, f32[112,256]{1,0:T(8,128)S(1)} %fusion.19.refs_2_.refs_3_, f32[112,256]{1,0:T(8,128)S(1)} %fusion.18.refs_4_, ...), custom_call_target="tpu_custom_call" | custom-call | tf_op jit(solution)/shard_map/pallas_call | solution.py:386
  99.3 2.6 %shard_map.238 = f32[12,96,128]{2,1,0:T(8,128)S(1)} custom-call(f32[8,24,256]{2,1,0:T(8,128)S(1)} %shard_map.237.refs_0_, f32[12,96,128]{2,1,0:T(8,128)S(1)} %pad.4.refs_1_, f32[96,128]{1,0:T(8,128)S(1)} %copy-done.5, f32[64,192]{1,0:T(8,128)S(1)} %copy-done.2, f32[128,256]{1,0:T(8,128)S(1)} %copy-done.1, f32[256,256]{1,0:T(8,128)S(1)} %copy-done), custom_call_target="tpu_custom_call" | custom-call | tf_op jit(solution)/shard_map/pallas_call | solution.py:274
  101.9 5.0 %shard_map.239 = f32[8,24,512]{2,1,0:T(8,128)} custom-call(s32[8,1,512]{2,1,0:T(1,128)S(1)} %get-tuple-element.31.cells_ref, f32[24,2048]{1,0:T(8,128)S(1)} %bitcast.41), custom_call_target="tpu_custom_call" | custom-call | tf_op jit(solution)/shard_map/pallas_call | solution.py:163
  106.9 4.5 %all-to-all-start = ((f32[8,24,512]{2,1,0:T(8,128)}), f32[8,24,512]{2,1,0:T(8,128)S(1)}, u32[]{:S(2)}, u32[]{:S(2)}) async-start(f32[8,24,512]{2,1,0:T(8,128)} %shard_map.239), calls=%async_computation | async-start | bytes 786432 | tf_op jit(solution)/shard_map/all_to_all | solution.py:427
  111.4 0.1 slice_subtract_fusion
  111.5 0.3 reshape.88
  111.8 0.1 collective-permute-start
  111.9 2.0 %collective-permute-done = f32[12,9216]{1,0:T(8,128)S(1)} collective-permute-done((f32[12,9216]{1,0:T(8,128)S(1)}, f32[12,9216]{1,0:T(8,128)S(1)}, u32[]{:S(2)}, u32[]{:S(2)}) %collective-permute-start) | collective-permute-done | bytes 442400 | tf_op jit(solution)/shard_map/ppermute | solution.py:412
  113.9 0.1 add.113
  114.0 1.6 %collective-permute-start.1 = (f32[12,9216]{1,0:T(8,128)S(1)}, f32[12,9216]{1,0:T(8,128)S(1)}, u32[]{:S(2)}, u32[]{:S(2)}) collective-permute-start(f32[12,9216]{1,0:T(8,128)S(1)} %add.113), channel_id=1, source_target_pairs={{0,16},{8,24},{16,0},{24,8},{1,17},{9,25},{17,1},{25,9},{2,18},{10... | collective-permute-start | bytes 1327112 | tf_op jit(solution)/shard_map/ppermute | solution.py:412
  115.6 5.0 %all-to-all-done = f32[8,24,512]{2,1,0:T(8,128)S(1)} async-done(((f32[8,24,512]{2,1,0:T(8,128)}), f32[8,24,512]{2,1,0:T(8,128)S(1)}, u32[]{:S(2)}, u32[]{:S(2)}) %all-to-all-start) | async-done | bytes 393248 | tf_op jit(solution)/shard_map/all_to_all | solution.py:427
  120.6 1.3 %multiply_add_fusion = (f32[8,12,512]{2,1,0:T(8,128)S(1)}, f32[8,12,512]{2,1,0:T(8,128)S(1)}) fusion(f32[8,24,512]{2,1,0:T(8,128)S(1)} %all-to-all-done, s32[512]{0:T(512)S(1)} %get-tuple-element.34, s32[8,12]{1,0:T(8,128)S(1)} %iota_add_fusion), kind=kLoop, calls=%fused_computation.23 | loop fusion | flops 786432 | bytes 788864 | tf_op jit(solution)/shard_map/add | solution.py:479
  122.0 0.6 fusion.30
  122.6 0.6 fusion.29
  123.2 0.6 fusion.1
  123.8 0.6 fusion.3
  124.4 0.8 maximum_bitcast_fusion
  125.3 4.2 %collective-permute-done.1 = f32[12,9216]{1,0:T(8,128)S(1)} collective-permute-done((f32[12,9216]{1,0:T(8,128)S(1)}, f32[12,9216]{1,0:T(8,128)S(1)}, u32[]{:S(2)}, u32[]{:S(2)}) %collective-permute-start.1) | collective-permute-done | bytes 442400 | tf_op jit(solution)/shard_map/ppermute | solution.py:412
  129.4 1.0 fusion.6
  (31 shorter events, 0.3 us)
Async XLA Ops:
  0.6 6.3 %copy-start.7 = (f32[128,96]{1,0:T(8,128)S(1)}, f32[128,96]{1,0:T(8,128)}, u32[]{:S(2)}) copy-start(f32[128,96]{1,0:T(8,128)} %constant.96.clone) | copy-start | bytes 147460
  0.6 5.4 %copy-start.9 = (f32[128,96]{1,0:T(8,128)S(1)}, f32[128,96]{1,0:T(8,128)}, u32[]{:S(2)}) copy-start(f32[128,96]{1,0:T(8,128)} %constant.95.clone) | copy-start | bytes 147460
  7.4 16.9 %copy-start.12 = (s32[112]{0:T(128)S(1)}, s32[112]{0:T(128)}, u32[]{:S(2)}) copy-start(s32[112]{0:T(128)} %constant.111) | copy-start | bytes 1348
  26.4 8.8 %copy-start = (f32[256,256]{1,0:T(8,128)S(1)}, f32[256,256]{1,0:T(8,128)}, u32[]{:S(2)}) copy-start(f32[256,256]{1,0:T(8,128)} %constant.103.clone.refs_5_) | copy-start | bytes 786436
  26.4 8.8 %copy-start.1 = (f32[128,256]{1,0:T(8,128)S(1)}, f32[128,256]{1,0:T(8,128)}, u32[]{:S(2)}) copy-start(f32[128,256]{1,0:T(8,128)} %constant.102.clone.refs_4_) | copy-start | bytes 393220
  26.4 8.8 %copy-start.2 = (f32[64,192]{1,0:T(8,128)S(1)}, f32[64,192]{1,0:T(8,128)}, u32[]{:S(2)}) copy-start(f32[64,192]{1,0:T(8,128)} %constant.101.clone.refs_3_) | copy-start | bytes 147460
  26.4 8.8 %copy-start.5 = (f32[96,128]{1,0:T(8,128)S(1)}, f32[96,128]{1,0:T(8,128)}, u32[]{:S(2)}) copy-start(f32[96,128]{1,0:T(8,128)} %constant.100.clone.refs_2_) | copy-start | bytes 147460
  26.5 13.0 %copy-start.3 = (f32[112,192]{1,0:T(8,128)S(1)}, f32[112,192]{1,0:T(8,128)}, u32[]{:S(2)}) copy-start(f32[112,192]{1,0:T(8,128)} %constant.105.clone.refs_6_) | copy-start | bytes 258052
  26.5 13.0 %copy-start.4 = (f32[192,112]{1,0:T(8,128)S(1)}, f32[192,112]{1,0:T(8,128)}, u32[]{:S(2)}) copy-start(f32[192,112]{1,0:T(8,128)} %constant.104.clone.refs_5_) | copy-start | bytes 258052
  106.9 13.7 %all-to-all-start = ((f32[8,24,512]{2,1,0:T(8,128)}), f32[8,24,512]{2,1,0:T(8,128)S(1)}, u32[]{:S(2)}, u32[]{:S(2)}) async-start(f32[8,24,512]{2,1,0:T(8,128)} %shard_map.239), calls=%async_computation | async-start | bytes 786432 | tf_op jit(solution)/shard_map/all_to_all | solution.py:427
  111.5 10.5 %copy-start.10 = (f32[128,96]{1,0:T(8,128)S(1)}, f32[128,96]{1,0:T(8,128)}, u32[]{:S(2)}) copy-start(f32[128,96]{1,0:T(8,128)} %constant.95.clone) | copy-start | bytes 147460
  111.8 11.4 %copy-start.8 = (f32[128,96]{1,0:T(8,128)S(1)}, f32[128,96]{1,0:T(8,128)}, u32[]{:S(2)}) copy-start(f32[128,96]{1,0:T(8,128)} %constant.96.clone) | copy-start | bytes 147460
  111.8 11.4 %copy-start.11 = (s32[512]{0:T(512)S(1)}, s32[512]{0:T(512)}, u32[]{:S(2)}) copy-start(s32[512]{0:T(512)} %param.26) | copy-start | bytes 6148
  111.8 2.1 %collective-permute-start = (f32[12,9216]{1,0:T(8,128)S(1)}, f32[12,9216]{1,0:T(8,128)S(1)}, u32[]{:S(2)}, u32[]{:S(2)}) collective-permute-start(f32[12,9216]{1,0:T(8,128)S(1)} %reshape.88), channel_id=1, source_target_pairs={{0,8},{8,0},{16,24},{24,16},{1,9},{9,1},{17,25},{25,17},{2,10},{10... | collective-permute-start | bytes 1327112 | tf_op jit(solution)/shard_map/ppermute | solution.py:412
  114.0 15.4 %collective-permute-start.1 = (f32[12,9216]{1,0:T(8,128)S(1)}, f32[12,9216]{1,0:T(8,128)S(1)}, u32[]{:S(2)}, u32[]{:S(2)}) collective-permute-start(f32[12,9216]{1,0:T(8,128)S(1)} %add.113), channel_id=1, source_target_pairs={{0,16},{8,24},{16,0},{24,8},{1,17},{9,25},{17,1},{25,9},{2,18},{10... | collective-permute-start | bytes 1327112 | tf_op jit(solution)/shard_map/ppermute | solution.py:412
  122.0 7.5 %copy-start.6 = (f32[12,9216]{1,0:T(8,128)S(1)}, f32[12,9216]{1,0:T(8,128)}, u32[]{:S(2)}) copy-start(f32[12,9216]{1,0:T(8,128)} %param.24) | copy-start | bytes 1327108
